TPU v7x, 256 devices: a whole 4x4x8 slice. The times are simulated.
256 devices in a mesh: ctx: 32 (over z, x), tp: 8 (over y, core).
Axes of the slice: x: 4, y: 4, z: 8, core: 2. Of those that a mesh axis runs over, the one named last changes fastest.
Arguments:
- mixer_input: bfloat16 [8192, 16384], P('ctx', 'tp'), may hold values from -6 to 6
- gate_input: bfloat16 [8192, 16384], P('ctx', 'tp'), may hold values from -6 to 6
- input_map: bfloat16 [8192, 2048], P('ctx', 'tp'), may hold values from -2 to 2
- output_map: bfloat16 [8192, 2048], P('ctx', 'tp'), may hold values from -2 to 2
- step_raw: float32 [256, 8192], P('tp', 'ctx'), may hold values from -4 to 4
- step_bias: float32 [256], P('tp'), may hold values from -4 to -1
- decay_log: float32 [256], P('tp'), may hold values from -7 to 0.7
- skip_gain: float32 [256], P('tp'), may hold values from 0.1 to 1.9
- norm_gain: float32 [16384], P('tp'), may hold values from 0.1 to 1.9
- queries: bfloat16 [8192, 8192], P('ctx', 'tp'), may hold values from -6 to 6
- key_heads: bfloat16 [8192, 1024], P('ctx', 'tp'), may hold values from -6 to 6
- value_heads: bfloat16 [8192, 1024], P('ctx', 'tp'), may hold values from -6 to 6
- out_weight: bfloat16 [8192, 4096], P('tp'), may hold values from -0.0625 to 0.0625
- rollout_lengths: int32 [4], replicated, may hold values from 1 to 4096, 8192 in all
Outputs:
- mamba_out: bfloat16 [8192, 16384], P('ctx', 'tp')
- block_out: bfloat16 [8192, 4096], P('ctx', 'tp')
Inputs may be any that keep to these rules, and one draw needn't show every extreme that they name: `rollout_lengths`: the longest rollout has exactly 4096 tokens; the lengths sum to 8192.
All inputs are finite; a program needn't handle non-finite values.
Results may differ from a plain program's by a relative error of at most 0.0075.
Values may be sent and summed in bfloat16 or wider, within the bound.
No kernel may reach another device: no remote copies, remote signals or barrier semaphores. Data moves between devices by JAX's collectives and lax.ppermute only.
A program may use at most 192 MiB of HBM per device.

v0:
```python
import math

import jax
import jax.numpy as jnp
from jax import lax
from jax.sharding import PartitionSpec as P

HEAD_P = 64
STATE = 256
HEAD_DIM = 128
SPAN = 128


norm_eps = 1e-05
big_negative = -1e30


def carried_in(part, axis, combine, identity):
    place = lax.axis_index(axis)
    gathered = jax.tree.map(lambda a: lax.all_gather(a, axis), part)
    state = jax.tree.map(lambda a, e: jnp.zeros_like(a) + jnp.asarray(e, a.dtype), part, identity)

    def one(hop, state):
        return combine(
            state, jax.tree.map(lambda a: lax.dynamic_index_in_dim(a, hop, 0, False), gathered)
        )

    return lax.fori_loop(0, place, one, state)


def rollout_of(index, lengths):
    ends = jnp.cumsum(lengths)
    counted = jnp.sum((index[:, None] >= ends[None, :]).astype(jnp.int32), axis=1)
    return jnp.where(index < 0, jnp.int32(-1), counted)


def span_step(state, parts):
    mixer_block, in_block, out_block, width_block, rate_block, seg_block, seg_prev = parts
    heads_here, state_dim, head_width = state.shape
    span_len = mixer_block.shape[0]
    groups_here = in_block.shape[1] // state_dim
    per_group = heads_here // groups_here
    cum = jnp.cumsum(rate_block, axis=1)
    order = jnp.arange(span_len)
    same = (seg_block[:, None] == seg_block[None, :]) & (order[:, None] >= order[None, :])
    diff = cum[:, :, None] - cum[:, None, :]
    decay = jnp.where(same[None], jnp.exp(jnp.where(same[None], diff, 0.0)), 0.0)
    in_g = in_block.reshape(span_len, groups_here, state_dim)
    out_g = out_block.reshape(span_len, groups_here, state_dim)
    inner = jnp.einsum("ign,jgn->gij", out_g, in_g, preferred_element_type=jnp.float32)
    mix = (
        decay.reshape(groups_here, per_group, span_len, span_len)
        * inner[:, None]
        * width_block.reshape(groups_here, per_group, 1, span_len)
    ).astype(jnp.bfloat16)
    mixer_g = mixer_block.reshape(span_len, groups_here, per_group, head_width)
    result = jnp.einsum("gkij,jgkp->igkp", mix, mixer_g, preferred_element_type=jnp.float32)
    kept = (seg_block == seg_prev).astype(jnp.float32)
    lead = (jnp.exp(cum) * kept[None, :]).T.reshape(span_len, groups_here, per_group, 1)
    carried = jnp.einsum(
        "ign,gknp->igkp",
        out_g.astype(jnp.float32),
        state.reshape(groups_here, per_group, state_dim, head_width),
        precision=lax.Precision.HIGHEST,
    )
    result = result + lead * carried
    last = cum[:, -1]
    tail = (
        jnp.where((seg_block == seg_block[-1])[None, :], jnp.exp(last[:, None] - cum), 0.0)
        * width_block
    )
    feed = (
        in_g[:, :, None, :]
        * tail.reshape(groups_here, per_group, span_len).transpose(2, 0, 1)[..., None]
    ).astype(jnp.bfloat16)
    fresh = jnp.einsum(
        "sgkn,sgkp->gknp", feed, mixer_g, preferred_element_type=jnp.float32
    ).reshape(heads_here, state_dim, head_width)
    through = jnp.where(seg_block[-1] == seg_prev, jnp.exp(last), 0.0)
    return (
        through[:, None, None] * state + fresh,
        result.reshape(span_len, heads_here * head_width),
    )


def chain_join(earlier, later):
    return (earlier[0] * later[0], later[0][:, None, None] * earlier[1] + later[1])


def body(
    mixer_input,
    gate_input,
    input_map,
    output_map,
    step_raw,
    step_bias,
    decay_log,
    skip_gain,
    norm_gain,
    queries,
    key_heads,
    value_heads,
    out_weight,
    rollout_lengths,
):
    tokens_here = mixer_input.shape[0]
    heads_here = step_raw.shape[0]
    groups_here = input_map.shape[1] // STATE
    per_group = heads_here // groups_here
    device_first = lax.axis_index("ctx") * tokens_here
    positions = device_first + jnp.arange(tokens_here, dtype=jnp.int32)
    rollout = rollout_of(positions, rollout_lengths)
    rollout_before = rollout_of(jnp.reshape(device_first - 1, (1,)), rollout_lengths)[0]
    width = jax.nn.softplus(step_raw + step_bias[:, None])
    rate = -jnp.exp(decay_log)[:, None] * width
    count = tokens_here // SPAN
    seg_blocks = rollout.reshape(count, SPAN)
    seg_prev = jnp.concatenate([jnp.reshape(rollout_before, (1,)), seg_blocks[:-1, -1]])
    parts = (
        mixer_input.reshape(count, SPAN, -1),
        input_map.reshape(count, SPAN, -1),
        output_map.reshape(count, SPAN, -1),
        width.reshape(heads_here, count, SPAN).transpose(1, 0, 2),
        rate.reshape(heads_here, count, SPAN).transpose(1, 0, 2),
        seg_blocks,
        seg_prev,
    )
    start_state = jnp.zeros((heads_here, STATE, HEAD_P), jnp.float32)
    final_state, blocks = lax.scan(span_step, start_state, parts)
    cum_all = jnp.cumsum(rate, axis=1)
    through_all = jnp.where(rollout[-1] == rollout_before, jnp.exp(cum_all[:, -1]), 0.0)
    chained = carried_in(
        (through_all, final_state),
        "ctx",
        chain_join,
        (jnp.ones_like(through_all), jnp.zeros_like(final_state)),
    )
    incoming = chained[1]
    lead = (jnp.exp(cum_all) * (rollout == rollout_before).astype(jnp.float32)[None, :]).T.reshape(
        tokens_here, groups_here, per_group, 1
    )
    carried = jnp.einsum(
        "tgn,gknp->tgkp",
        output_map.reshape(tokens_here, groups_here, STATE).astype(jnp.float32),
        incoming.reshape(groups_here, per_group, STATE, HEAD_P),
        precision=lax.Precision.HIGHEST,
    )
    mixed = blocks.reshape(tokens_here, groups_here, per_group, HEAD_P) + lead * carried
    mixed = mixed.reshape(tokens_here, heads_here, HEAD_P) + skip_gain[
        None, :, None
    ] * mixer_input.reshape(tokens_here, heads_here, HEAD_P).astype(jnp.float32)
    gated = mixed.reshape(tokens_here, heads_here * HEAD_P) * jax.nn.silu(
        gate_input.astype(jnp.float32)
    )
    grouped = gated.reshape(tokens_here, groups_here, -1)
    factor = lax.rsqrt(jnp.mean(grouped * grouped, axis=2, keepdims=True) + norm_eps)
    mamba_out = ((grouped * factor).reshape(tokens_here, -1) * norm_gain[None, :]).astype(
        jnp.bfloat16
    )
    kv_here = key_heads.shape[1] // HEAD_DIM
    group_size = queries.shape[1] // HEAD_DIM // kv_here
    query_split = queries.reshape(tokens_here, kv_here, group_size, HEAD_DIM)
    scale = 1.0 / math.sqrt(HEAD_DIM)

    def absorb(carry, key_block, value_block, start):
        rows = key_block.shape[0]
        key_index = start + jnp.arange(rows, dtype=jnp.int32)
        key_roll = rollout_of(key_index, rollout_lengths)
        visible = (rollout[:, None] == key_roll[None, :]) & (
            positions[:, None] >= key_index[None, :]
        )

        def compute(state):
            peak, total, summed = state
            logits = (
                jnp.einsum(
                    "tkgd,skd->kgts",
                    query_split,
                    key_block.reshape(rows, kv_here, HEAD_DIM),
                    preferred_element_type=jnp.float32,
                )
                * scale
            )
            masked = jnp.where(visible[None, None], logits, big_negative)
            fresh = jnp.maximum(peak, jnp.max(masked, axis=3))
            factor_old = jnp.exp(peak - fresh)
            weights = jnp.where(visible[None, None], jnp.exp(masked - fresh[..., None]), 0.0)
            total = total * factor_old + jnp.sum(weights, axis=3)
            summed = summed * factor_old[..., None] + jnp.einsum(
                "kgts,skd->kgtd",
                weights.astype(jnp.bfloat16),
                value_block.reshape(rows, kv_here, HEAD_DIM),
                preferred_element_type=jnp.float32,
            )
            return (fresh, total, summed)

        def keep_state(state):
            return state

        return lax.cond(jnp.any(visible), compute, keep_state, carry)

    start_carry = (
        jnp.full((kv_here, group_size, tokens_here), big_negative, jnp.float32),
        jnp.zeros((kv_here, group_size, tokens_here), jnp.float32),
        jnp.zeros((kv_here, group_size, tokens_here, HEAD_DIM), jnp.float32),
    )
    carry = start_carry
    key_piece = lax.all_gather(key_heads, "ctx", axis=0, tiled=True)
    value_piece = lax.all_gather(value_heads, "ctx", axis=0, tiled=True)
    rows = key_piece.shape[0]
    sub_rows = math.gcd(rows, 1024)
    pieces = rows // sub_rows

    def inner_step(state, items):
        key_sub, value_sub, offset = items
        return (absorb(state, key_sub, value_sub, offset * sub_rows), None)

    carry, ignored = lax.scan(
        inner_step,
        carry,
        (
            key_piece.reshape(pieces, sub_rows, -1),
            value_piece.reshape(pieces, sub_rows, -1),
            jnp.arange(pieces, dtype=jnp.int32),
        ),
    )
    peak, total, summed = carry
    attended = (
        (summed / total[..., None])
        .transpose(2, 0, 1, 3)
        .reshape(tokens_here, kv_here * group_size * HEAD_DIM)
        .astype(jnp.bfloat16)
    )
    projected = lax.psum_scatter(
        lax.dot_general(
            out_weight, attended, (((0,), (1,)), ((), ())), preferred_element_type=jnp.float32
        ),
        "tp",
        scatter_dimension=0,
        tiled=True,
    )
    block_out = projected.T.astype(jnp.bfloat16)
    return (mamba_out, block_out)


def solution(mesh):
    return jax.shard_map(
        body,
        mesh=mesh,
        in_specs=(
            P("ctx", "tp"),
            P("ctx", "tp"),
            P("ctx", "tp"),
            P("ctx", "tp"),
            P("tp", "ctx"),
            P("tp"),
            P("tp"),
            P("tp"),
            P("tp"),
            P("ctx", "tp"),
            P("ctx", "tp"),
            P("ctx", "tp"),
            P("tp", None),
            P(),
        ),
        out_specs=(P("ctx", "tp"), P("ctx", "tp")),
        check_vma=False,
    )
```

profile of v0, /device:TPU:230, one launch (start us, length us, event | category | flops | bytes accessed | tf_op | source)
XLA Modules:
  0.0 1103.2 jit_solution(3251138869144282315)
XLA Ops:
  13.3 72.5 %all-gather.6.cloned.1.call-done = bf16[8192,128]{1,0:T(8,128)(2,1)} async-done(((bf16[256,128]{1,0:T(8,128)(2,1)}), bf16[8192,128]{1,0:T(8,128)(2,1)}) %all-gather.6.cloned.1.call-update) | async-done | bytes 2097168 | tf_op jit(solution)/shard_map/all_gather | solution.py:208
  85.8 77.7 %all-gather.8.cloned.1.call-done = bf16[8192,128]{1,0:T(8,128)(2,1)} async-done(((bf16[256,128]{1,0:T(8,128)(2,1)}), bf16[8192,128]{1,0:T(8,128)(2,1)}) %all-gather.8.cloned.1.call-update) | async-done | bytes 2097168 | tf_op jit(solution)/shard_map/all_gather | solution.py:209
  163.6 49.0 %while.43 = (s32[]{:T(128)}, f32[1,8,256]{2,1,0:T(8,128)S(1)}, f32[1,8,256]{2,1,0:T(8,128)S(1)}, f32[1,8,256,128]{3,2,1,0:T(8,128)S(1)}, s32[256]{0:T(256)S(1)},...) while((s32[]{:T(128)}, f32[1,8,256]{2,1,0:T(8,128)S(1)}, ...), condition=%wide.region_19.20_spmd.clone, body=%wide.region_12.19_spmd.clone.sunk | while | flops 1102599424 | bytes 29524280 | solution.py:218
  182.2 8.1 conditional.3
  186.6 3.6 fusion.12
  193.3 8.1 conditional.3
  197.8 3.6 fusion.12
  204.5 8.1 conditional.3
  208.9 3.6 fusion.12
  213.0 7.7 convolution_bitcast_fusion.1
  222.6 73.7 %while.44 = (s32[]{:T(128)}, f32[32,256,64]{1,2,0:T(8,128)}, f32[2,128,2048]{1,0,2:T(2,128)}, s32[2,128]{1,0:T(2,128)S(1)}, s32[2]{0:T(128)S(1)}, /*index=5*/f32...) while((s32[]{:T(128)}, f32[32,256,64]{1,2,0:T(8,128)}, ...), condition=%wide.region_5.6_spmd.clone, body=%wide.region_3.5_spmd.clone.sunk | while | flops 1022980480 | bytes 24007916 | solution.py:129
  233.1 26.0 %dynamic_update_slice.6 = f32[2,128,2048]{1,0,2:T(2,128)} dynamic-update-slice(f32[2,128,2048]{1,0,2:T(2,128)} %get-tuple-element.748, f32[1,128,2048]{1,0,2:T(1,128)S(1)} %bitcast.234, s32[]{:T(128)S(6)} %copy.105, s32[]{:T(128)} %constant.128.clone.1..sunk.1, s32[]{:T(128)} %constant.128.clone.1..sunk.1) | dynamic-update-slice | bytes 2097156 | tf_op jit(solution)/shard_map/while/body/jit(dynamic_update_index_in_dim)/dynamic_update_slice | solution.py:129
  270.2 26.0 %dynamic_update_slice.6 = f32[2,128,2048]{1,0,2:T(2,128)} dynamic-update-slice(f32[2,128,2048]{1,0,2:T(2,128)} %get-tuple-element.748, f32[1,128,2048]{1,0,2:T(1,128)S(1)} %bitcast.234, s32[]{:T(128)S(6)} %copy.105, s32[]{:T(128)} %constant.128.clone.1..sunk.1, s32[]{:T(128)} %constant.128.clone.1..sunk.1) | dynamic-update-slice | bytes 2097156 | tf_op jit(solution)/shard_map/while/body/jit(dynamic_update_index_in_dim)/dynamic_update_slice | solution.py:129
  303.7 70.2 %all-reduce = f32[1024]{0:T(1024)S(1)} all-reduce(f32[1024]{0:T(1024)S(1)} %dynamic-update-slice), channel_id=2, replica_groups=mesh['ctx'=32,'tp'=8] {'ctx'}, use_global_device_ids=true, to_apply=%add | all-reduce | flops 1024 | bytes 8192
  376.1 364.5 %all-gather.10.cloned.1.call-done = f32[1024,256,64]{1,2,0:T(8,128)} async-done(((f32[32,256,64]{1,2,0:T(8,128)}), f32[1024,256,64]{1,2,0:T(8,128)}) %all-gather.10.cloned.1.call-update) | async-done | bytes 67108880 | tf_op jit(solution)/shard_map/all_gather | solution.py:20
  743.0 340.6 %while.42 = (s32[]{:T(128)}, f32[32,256,64]{2,1,0:T(8,128)}, s32[]{:T(128)}, f32[32,32]{1,0:T(8,128)S(1)}, f32[32,32,256,64]{2,3,1,0:T(8,128)}, /*index=5*/s32[]{:T(128)}, s32[]{:T(128)}, s32[]{:T(128)}) while((s32[]{:T(128)}, f32[32,256,64]{2,1,0:T(8,128)}, s32[]{:T(128)}, f32[32,32]{1,0:T(8,128)S(1)}, f32[32,32,256,64]{2,3,1,0:T(8,128)}, ...), condition=%wide.region_9.10_spmd, body=%wide.region_8.9_spmd.sunk | while | flops 1048581 | bytes 14680583 | solution.py:28
  744.8 2.7 copy.93
  747.5 6.5 bitcast_add_fusion.3
  755.8 2.7 copy.93
  758.5 6.5 bitcast_add_fusion.3
  766.7 2.7 copy.93
  769.4 6.5 bitcast_add_fusion.3
  780.4 6.5 bitcast_add_fusion.3
  788.7 2.7 copy.93
  791.4 6.5 bitcast_add_fusion.3
  802.4 6.5 bitcast_add_fusion.3
  813.4 6.5 bitcast_add_fusion.3
  821.7 2.7 copy.93
  824.4 6.5 bitcast_add_fusion.3
  835.4 6.5 bitcast_add_fusion.3
  843.7 2.7 copy.93
  846.4 6.5 bitcast_add_fusion.3
  857.3 6.5 bitcast_add_fusion.3
  865.6 2.7 copy.93
  868.3 6.5 bitcast_add_fusion.3
  876.6 2.7 copy.93
  879.3 6.5 bitcast_add_fusion.3
  890.3 6.5 bitcast_add_fusion.3
  898.6 2.7 copy.93
  901.3 6.5 bitcast_add_fusion.3
  912.3 6.5 bitcast_add_fusion.3
  920.6 2.7 copy.93
  923.3 6.5 bitcast_add_fusion.3
  934.3 6.5 bitcast_add_fusion.3
  945.2 6.5 bitcast_add_fusion.3
  953.5 2.7 copy.93
  956.2 6.5 bitcast_add_fusion.3
  967.2 6.5 bitcast_add_fusion.3
  975.5 2.7 copy.93
  978.2 6.5 bitcast_add_fusion.3
  989.2 6.5 bitcast_add_fusion.3
  997.5 2.7 copy.93
  1000.2 6.5 bitcast_add_fusion.3
  1011.2 6.5 bitcast_add_fusion.3
  1022.2 6.5 bitcast_add_fusion.3
  1030.4 2.7 copy.93
  1033.1 6.5 bitcast_add_fusion.3
  1044.1 6.5 bitcast_add_fusion.3
  1052.4 2.7 copy.93
  1055.1 6.5 bitcast_add_fusion.3
  1066.1 6.5 bitcast_add_fusion.3
  1074.4 2.7 copy.93
  1077.1 6.5 bitcast_add_fusion.3
  1083.6 7.7 fusion.58
  (261 shorter events, 166.1 us)
Async XLA Ops:
  7.2 78.6 %all-gather.6.cloned.1.call-start = ((), (), s32[]{:S(2)}) async-start(), calls=%async_computation.1 | async-start | bytes 2162688 | tf_op jit(solution)/shard_map/all_gather | solution.py:208
  7.9 155.6 %all-gather.8.cloned.1.call-start = ((), (), s32[]{:S(2)}) async-start(), calls=%async_computation.2 | async-start | bytes 2162688 | tf_op jit(solution)/shard_map/all_gather | solution.py:209
  8.6 365.6 %reduce-scatter.2.cloned.1.call-start = ((), (), s32[]{:S(2)}) async-start(), calls=%async_computation.3 | async-start | bytes 4718592 | tf_op jit(solution)/shard_map/reduce_scatter | solution.py:234
  220.8 0.9 copy-start.9
  220.8 1.0 copy-start.5
  220.8 1.0 copy-start.7
  220.8 1.8 copy-start.2
  220.8 1.8 copy-start.3
  220.8 519.7 %all-gather.10.cloned.1.call-start = ((), (), s32[]{:S(2)}) async-start(), calls=%async_computation.4 | async-start | bytes 69206016 | tf_op jit(solution)/shard_map/all_gather | solution.py:20
  222.6 1.2 copy-start
  259.1 1.9 copy-start
  296.2 1.6 copy-start.4
  297.8 4.1 copy-start.10
  297.8 76.2 %copy-start.8 = (f32[32]{0:T(128)S(1)}, f32[32]{0:T(128)}, u32[]{:S(2)}) copy-start(f32[32]{0:T(128)} %param.29) | copy-start | bytes 388
  1091.3 2.0 copy-start.1
  1093.3 2.1 copy-start.6
Sparse Core Ops, SparseCore 0:
  10.6 75.1 all-gather.5
  88.4 75.1 all-gather.7
  220.9 56.8 reduce-scatter.1
  296.4 444.1 all-gather.9
where the time goes:
time: 1110 us; the launch traced here: 1100 us
  waiting for transfers between devices  516 us (46%)
  other arithmetic  234 us (21%)
  local copies, waits for them, and re-layouts  212 us (19%)
  blocking collectives  70.2 us (6%)
  matrix products  42 us (4%)
  between operations  15.9 us (1%)
  loops' own time  12.5 us (1%)
    all_gather x1, waiting for transfers between devices, carried_in(): gathered = jax.tree.map(lambda a: lax.all_gather(a, axis), part)  364 us
    add x31, other arithmetic, chain_join(): later[0][:, None, None] * earlier[1] + later[1]  202 us
    dynamic_slice x62, local copies, waits for them, and re-layouts, one(): lax.dynamic_index_in_dim(a, hop, 0, False)  138 us
    all_gather x1, waiting for transfers between devices, body(): value_piece = lax.all_gather(value_heads, 'ctx', axis=0, tiled=True)  77.7 us
    all_gather x1, waiting for transfers between devices, body(): key_piece = lax.all_gather(key_heads, 'ctx', axis=0, tiled=True)  72.5 us
    unnamed x1, blocking collectives  70.2 us
    dynamic_update_slice x2, local copies, waits for them, and re-layouts, body(): final_state, blocks = lax.scan(span_step, start_state, parts)  52 us
  transfers between devices with their start and end apart: 4, of which 3 were waited for; matrix products, arithmetic and copies ran while one was open for 7% of the time, Pallas kernels for 0%

commit v1 on v0

v1 whole, which is shorter than its diff:
```python
import math

import jax
import jax.numpy as jnp
from jax import lax
from jax.experimental import pallas as pl
from jax.experimental.pallas import tpu as pltpu
from jax.sharding import PartitionSpec as P

HEAD_P = 64
STATE = 256
HEAD_DIM = 128
NZ = 8
NX = 4
NY = 4
LOG2E = math.log2(math.e)
EPS = 1e-05
BIG = -1e30
F32 = jnp.float32
BF16 = jnp.bfloat16
EXTRA = 16
QUARTER = 512


def iota(shape, dim):
    return lax.broadcasted_iota(jnp.int32, shape, dim)


def split3(a):
    hi = a.astype(BF16)
    rest = a - hi.astype(F32)
    mid = rest.astype(BF16)
    low = (rest - mid.astype(F32)).astype(BF16)
    return hi, mid, low


def spread(a, expand, terms=3):
    total = None
    for part in split3(a)[:terms]:
        one = jnp.dot(part, expand, preferred_element_type=F32)
        total = one if total is None else total + one
    return total


def expander(heads, lanes):
    return (iota((heads, lanes), 1) // HEAD_P == iota((heads, lanes), 0)).astype(F32).astype(BF16)


def ends_of(lengths):
    e0 = lengths[0]
    e1 = e0 + lengths[1]
    e2 = e1 + lengths[2]
    return e0, e1, e2, e2 + lengths[3]


def rollout_at(pos, ends):
    count = jnp.zeros_like(pos)
    for e in ends:
        count = count + (pos >= e).astype(jnp.int32)
    return jnp.where(pos < 0, -1, count)


def state_kernel(place, lengths, x_ref, b_ref, raw_ref, bias_ref, alog_ref,
                 o0, o1, o2, o3, d_ref, cumt_ref, lead_ref, scr):
    heads, toks = raw_ref.shape
    lanes = x_ref.shape[1]
    zi, xi = place[0], place[1]
    first = (zi * NX + xi) * toks
    ends = ends_of(lengths)
    width = jax.nn.softplus(raw_ref[...] + bias_ref[...])
    rate2 = (-LOG2E * jnp.exp(alog_ref[...])) * width
    upper = (iota((toks, toks), 0) <= iota((toks, toks), 1)).astype(F32)
    cum = jnp.dot(rate2, upper, precision=lax.Precision.HIGHEST, preferred_element_type=F32)
    cumt = cum.T
    width_t = width.T
    d_ref[...] = cum - jnp.log2(width)
    cumt_ref[...] = cumt
    before = rollout_at(first - 1, ends)
    last = rollout_at(first + (toks - 1), ends)
    roll = rollout_at(first + iota((toks, heads), 0), ends)
    lead_ref[...] = jnp.where(roll == before, jnp.exp2(cumt), 0.0)
    end = cumt[toks - 1:toks, :]
    tail = jnp.where(roll == last, jnp.exp2(end - cumt), 0.0) * width_t
    expand = expander(heads, lanes)
    xw = (spread(tail, expand, 2) * x_ref[...].astype(F32)).astype(BF16)
    state = lax.dot_general(b_ref[...], xw, (((0,), (0,)), ((), ())), preferred_element_type=F32)
    through = jnp.where(last == before, jnp.exp2(end), 0.0)
    th = [jnp.dot(part, expand, preferred_element_type=F32) for part in split3(through)]
    row = iota((EXTRA, lanes), 0)
    extra = jnp.where(row == 0, th[0], jnp.where(row == 1, th[1], jnp.where(row == 2, th[2], 0.0)))
    whole = jnp.concatenate([state, extra], axis=0).astype(BF16)
    for q in range(NX):
        scr[q] = whole[:, q * QUARTER:(q + 1) * QUARTER]
    for k, out in enumerate((o0, o1, o2, o3)):
        out[...] = scr[lax.rem(xi + k, NX)]


def row_kernel(place, a0, a1, a2, a3, p_ref, t_ref, pth_ref, th_ref, scr):
    xi = place[1]
    for k, a in enumerate((a0, a1, a2, a3)):
        scr[lax.rem(xi - k + NX, NX)] = a[...]
    total = jnp.zeros((STATE, QUARTER), F32)
    through = jnp.ones((1, QUARTER), F32)
    for j in range(NX):
        p_ref[j] = total.astype(BF16)
        pth_ref[j] = jnp.broadcast_to(through, (8, QUARTER))
        tail = scr[j, STATE:STATE + EXTRA, :].astype(F32)
        one = tail[0:1] + tail[1:2] + tail[2:3]
        total = one * total + scr[j, :STATE, :].astype(F32)
        through = through * one
    t_ref[...] = total.astype(BF16)
    th_ref[...] = jnp.broadcast_to(through, (8, QUARTER))


def back_kernel(place, p_ref, pth_ref, r_ref, o0, o1, o2, o3):
    xi = place[1]
    came = r_ref[...].astype(F32)
    for k, out in enumerate((o0, o1, o2, o3)):
        j = lax.rem(xi + k, NX)
        out[...] = (p_ref[j].astype(F32) + pth_ref[j][0:1] * came).astype(BF16)


def local_kernel(place, lengths, x_ref, b_ref, c_ref, d_ref, cumt_ref, skip_ref, y_ref):
    toks, lanes = x_ref.shape
    heads = d_ref.shape[0]
    half = toks // 2
    first = (place[0] * NX + place[1]) * toks
    ends = ends_of(lengths)
    roll_t = rollout_at(first + iota((toks, toks), 0), ends)
    roll_s = rollout_at(first + iota((toks, toks), 1), ends)
    seen = (roll_t == roll_s) & (iota((toks, toks), 0) >= iota((toks, toks), 1))
    inner = lax.dot_general(c_ref[...], b_ref[...], (((1,), (1,)), ((), ())), preferred_element_type=F32)
    inner = jnp.where(seen, inner, 0.0)
    left = iota((half, 128), 1) < HEAD_P
    skip = spread(skip_ref[...], expander(heads, lanes))
    d_all = d_ref[...]
    cumt = cumt_ref[...]
    for pair in range(heads // 2):
        cols = slice(pair * 128, (pair + 1) * 128)
        x_pair = x_ref[:, cols]
        for rows, width in ((slice(0, half), half), (slice(half, toks), toks)):
            res = []
            for h in (2 * pair, 2 * pair + 1):
                diff = cumt[rows, h:h + 1] - d_all[h:h + 1, :width]
                mix = (jnp.exp2(jnp.minimum(diff, 64.0)) * inner[rows, :width]).astype(BF16)
                res.append(jnp.dot(mix, x_pair[:width], preferred_element_type=F32))
            y_ref[rows, cols] = jnp.where(left, res[0], res[1]) + skip[:, cols] * x_pair[rows].astype(F32)


def gate_kernel(place, y_ref, c_ref, lead_ref, gate_ref, gain_ref, i0, i1, i2, i3, out_ref, scr):
    toks, lanes = y_ref.shape
    heads = lead_ref.shape[1]
    xi = place[1]
    for k, a in enumerate((i0, i1, i2, i3)):
        scr[lax.rem(xi - k + NX, NX)] = a[...]
    expand = expander(heads, lanes)
    square = jnp.zeros((toks, 1), F32)
    held = []
    for q in range(NX):
        cols = slice(q * QUARTER, (q + 1) * QUARTER)
        carried = jnp.dot(c_ref[...], scr[q], preferred_element_type=F32)
        lead = spread(lead_ref[...], expand[:, cols], 2)
        v = gate_ref[:, cols].astype(F32)
        gated = (y_ref[:, cols] + lead * carried) * (v / (1.0 + jnp.exp(-v)))
        square = square + jnp.sum(gated * gated, axis=1, keepdims=True)
        held.append(gated)
    factor = lax.rsqrt(square * (1.0 / lanes) + EPS)
    for q in range(NX):
        cols = slice(q * QUARTER, (q + 1) * QUARTER)
        out_ref[:, cols] = (held[q] * factor * gain_ref[:, cols]).astype(BF16)


def attend_kernel(place, lengths, q_ref, own, z1, z2, z3, z4, g1, g2, g3, out_ref,
                  k_buf, v_buf, q_buf, s_a, s_b):
    toks = q_ref.shape[0]
    heads = q_ref.shape[1] // HEAD_DIM
    chunks = k_buf.shape[0]
    zi, xi = place[0], place[1]
    first = (zi * NX + xi) * toks
    ends = ends_of(lengths)
    lane = iota((toks, HEAD_DIM), 1)
    ones = (lane == 0).astype(F32).astype(BF16)

    def put(slot, kv):
        k_buf[slot, :, :HEAD_DIM] = kv[:, :HEAD_DIM]
        v_buf[slot, :, :HEAD_DIM] = kv[:, HEAD_DIM:]

    put(16, own)
    for r, a in ((1, z1), (2, z2), (3, z3), (4, z4)):
        put(16 - 4 * r, a)
    for k, g in ((1, g1), (2, g2), (3, g3)):
        ahead = xi >= k
        put(jnp.where(ahead, 16 - k, 4 - k), g[0:toks, :])
        for r in (1, 2, 3):
            put(jnp.where(ahead, 16 - 4 * r - k, 20 - 4 * r - k), g[r * toks:(r + 1) * toks, :])
    for j in range(chunks):
        pos = first + (j - (chunks - 1)) * toks + iota((toks, HEAD_DIM), 0)
        k_buf[j, :, HEAD_DIM:] = jnp.where(rollout_at(pos, ends) == lane, 0.0, BIG).astype(BF16)
        v_buf[j, :, HEAD_DIM:] = ones
    mine = (rollout_at(first + iota((toks, HEAD_DIM), 0), ends) == lane).astype(F32).astype(BF16)
    for h in range(heads):
        q_buf[h, :, :HEAD_DIM] = q_ref[:, h * HEAD_DIM:(h + 1) * HEAD_DIM]
        q_buf[h, :, HEAD_DIM:] = mine
    causal = iota((toks, toks), 0) >= iota((toks, toks), 1)
    scale = LOG2E / math.sqrt(HEAD_DIM)

    def scores(h, buf, j, peak):
        s = lax.dot_general(q_buf[h], k_buf[j], (((1,), (1,)), ((), ())), preferred_element_type=F32)
        if j == chunks - 1:
            s = jnp.where(causal, s, BIG)
        buf[j] = s
        return jnp.maximum(peak, jnp.maximum(s[:, :128], s[:, 128:]))

    def finish(h, acc):
        res = acc[:, :HEAD_DIM] / acc[:, HEAD_DIM:HEAD_DIM + 1]
        out_ref[h] = res.astype(BF16)

    def weigh(buf, j, top):
        p = jnp.exp2((buf[j] - top) * scale).astype(BF16)
        return jnp.dot(p, v_buf[j], preferred_element_type=F32)

    low = jnp.full((toks, 128), BIG, F32)
    peak = low
    for j in range(chunks):
        peak = scores(0, s_a, j, peak)

    def both(h, buf_now, buf_next, peak):
        top = jnp.max(peak, axis=1, keepdims=True)
        nxt = jnp.minimum(h + 1, heads - 1)
        peak = low
        acc = jnp.zeros((toks, 2 * HEAD_DIM), F32)
        for j in range(chunks):
            peak = scores(nxt, buf_next, j, peak)
            acc = acc + weigh(buf_now, j, top)
        finish(h, acc)
        return peak

    def two(i, peak):
        peak = both(2 * i, s_a, s_b, peak)
        return both(2 * i + 1, s_b, s_a, peak)

    lax.fori_loop(0, heads // 2, two, peak)


def project_kernel(place, a_ref, w_ref, out_ref, wide):
    h = a_ref.shape[0]

    @pl.when(pl.program_id(0) == 0)
    def _():
        for i in range(h):
            wide[:, i * HEAD_DIM:(i + 1) * HEAD_DIM] = a_ref[i]

    out_ref[0] = jnp.dot(wide[...], w_ref[...], preferred_element_type=F32).astype(BF16)


def vmem(n):
    return [pl.BlockSpec(memory_space=pltpu.VMEM)] * n


def smem(n):
    return [pl.BlockSpec(memory_space=pltpu.SMEM)] * n


def sds(shape, dtype):
    return jax.ShapeDtypeStruct(shape, dtype)


PARAMS = pltpu.CompilerParams(vmem_limit_bytes=56 * 1024 * 1024)


def x_shift(k):
    return [(NX * z + x, NX * z + (x + k) % NX) for z in range(NZ) for x in range(NX)]


def y_shift(k):
    return [(2 * y + c, 2 * ((y + k) % NY) + c) for y in range(NY) for c in range(2)]


Z_STEP = [(NX * z + x, NX * (z + 1) + x) for z in range(NZ - 1) for x in range(NX)]
TWIN = [(i, i ^ 1) for i in range(2 * NY)]


def body(mixer_input, gate_input, input_map, output_map, step_raw, step_bias, decay_log, skip_gain,
         norm_gain, queries, key_heads, value_heads, out_weight, rollout_lengths):
    toks, lanes = mixer_input.shape
    heads = step_raw.shape[0]
    ctx = lax.axis_index("ctx")
    tp = lax.axis_index("tp")
    zi, xi = ctx // NX, ctx % NX
    place = jnp.stack([zi, xi, tp // 2, tp % 2]).astype(jnp.int32)
    msg = sds((STATE + EXTRA, QUARTER), BF16)
    quarter = sds((STATE, QUARTER), BF16)

    own = jnp.concatenate([key_heads, value_heads], axis=1)
    zs = [own]
    for _ in range(4):
        zs.append(lax.ppermute(zs[-1], "ctx", Z_STEP))

    o0, o1, o2, o3, dd, cumt, lead = pl.pallas_call(
        state_kernel,
        in_specs=smem(2) + vmem(5),
        out_specs=vmem(7),
        out_shape=[msg] * 4 + [sds((heads, toks), F32), sds((toks, heads), F32), sds((toks, heads), F32)],
        scratch_shapes=[pltpu.VMEM((NX, STATE + EXTRA, QUARTER), BF16)],
        compiler_params=PARAMS,
        name="chunk_states",
    )(place, rollout_lengths, mixer_input, input_map, step_raw, step_bias[:, None], decay_log[:, None])
    came = [o0] + [lax.ppermute(o, "ctx", x_shift(k)) for k, o in ((1, o1), (2, o2), (3, o3))]
    prefix, total, pth, th = pl.pallas_call(
        row_kernel,
        in_specs=smem(1) + vmem(4),
        out_specs=vmem(4),
        out_shape=[sds((NX, STATE, QUARTER), BF16), quarter, sds((NX, 8, QUARTER), F32), sds((8, QUARTER), F32)],
        scratch_shapes=[pltpu.VMEM((NX, STATE + EXTRA, QUARTER), BF16)],
        compiler_params=PARAMS,
        name="row_scan",
    )(place, *came)

    gs = []
    for k in (1, 2, 3):
        edge = jnp.where(xi + k < NX, own, zs[4])
        gs.append(lax.ppermute(jnp.concatenate([edge, zs[1], zs[2], zs[3]], axis=0), "ctx", x_shift(k)))

    carry = lax.ppermute(total, "ctx", Z_STEP)
    for _ in range(3):
        carry = (total.astype(F32) + th[0:1] * carry.astype(F32)).astype(BF16)
        carry = lax.ppermute(carry, "ctx", Z_STEP)
    backs = pl.pallas_call(
        back_kernel,
        in_specs=smem(1) + vmem(3),
        out_specs=vmem(4),
        out_shape=[quarter] * 4,
        compiler_params=PARAMS,
        name="row_states",
    )(place, prefix, pth, carry)
    incoming = [backs[0]] + [lax.ppermute(backs[k], "ctx", x_shift(k)) for k in (1, 2, 3)]

    y_local = pl.pallas_call(
        local_kernel,
        in_specs=smem(2) + vmem(6),
        out_specs=pl.BlockSpec(memory_space=pltpu.VMEM),
        out_shape=sds((toks, lanes), F32),
        compiler_params=PARAMS,
        name="within_chunk",
    )(place, rollout_lengths, mixer_input, input_map, output_map, dd, cumt, skip_gain[None, :])

    q_heads = queries.shape[1] // HEAD_DIM
    window = 17
    attended = pl.pallas_call(
        attend_kernel,
        in_specs=smem(2) + vmem(9),
        out_specs=pl.BlockSpec(memory_space=pltpu.VMEM),
        out_shape=sds((q_heads, toks, HEAD_DIM), BF16),
        scratch_shapes=[
            pltpu.VMEM((window, toks, 2 * HEAD_DIM), BF16),
            pltpu.VMEM((window, toks, 2 * HEAD_DIM), BF16),
            pltpu.VMEM((q_heads, toks, 2 * HEAD_DIM), BF16),
            pltpu.VMEM((window, toks, toks), F32),
            pltpu.VMEM((window, toks, toks), F32),
        ],
        compiler_params=PARAMS,
        name="attend",
    )(place, rollout_lengths, queries, *zs, *gs)

    cols = out_weight.shape[1] // (2 * NY)

    def column(i, place):
        y = lax.rem(place[2] + lax.rem(i, NY), NY)
        core = jnp.where(i < NY, 1 - place[3], place[3])
        return (0, 2 * y + core)

    partial = pl.pallas_call(
        project_kernel,
        grid_spec=pltpu.PrefetchScalarGridSpec(
            num_scalar_prefetch=1,
            grid=(2 * NY,),
            in_specs=[
                pl.BlockSpec((q_heads, toks, HEAD_DIM), lambda i, place: (0, 0, 0)),
                pl.BlockSpec((out_weight.shape[0], cols), column),
            ],
            out_specs=pl.BlockSpec((1, toks, cols), lambda i, place: (i, 0, 0)),
            scratch_shapes=[pltpu.VMEM((toks, q_heads * HEAD_DIM), BF16)],
        ),
        out_shape=sds((2 * NY, toks, cols), BF16),
        compiler_params=PARAMS,
        name="project",
    )(place, attended, out_weight)
    twin = lax.ppermute(partial[:NY], "tp", TWIN)
    summed = [partial[NY + k].astype(F32) + twin[k].astype(F32) for k in range(NY)]
    block_out = summed[0]
    for k in (1, 2, 3):
        block_out = block_out + lax.ppermute(summed[k].astype(BF16), "tp", y_shift(k)).astype(F32)
    block_out = block_out.astype(BF16)

    mamba_out = pl.pallas_call(
        gate_kernel,
        in_specs=smem(1) + vmem(9),
        out_specs=pl.BlockSpec(memory_space=pltpu.VMEM),
        out_shape=sds((toks, lanes), BF16),
        scratch_shapes=[pltpu.VMEM((NX, STATE, QUARTER), BF16)],
        compiler_params=PARAMS,
        name="carry_gate_norm",
    )(place, y_local, output_map, lead, gate_input, norm_gain[None, :], *incoming)
    return (mamba_out, block_out)


def solution(mesh):
    both = P("ctx", "tp")
    return jax.shard_map(
        body,
        mesh=mesh,
        in_specs=(both, both, both, both, P("tp", "ctx"), P("tp"), P("tp"), P("tp"), P("tp"),
                  both, both, both, P("tp", None), P()),
        out_specs=(both, both),
        check_vma=False,
    )
```

time: 1110 us -> 154 us (0.14)
  the two profiles are of different devices: /device:TPU:230 before, /device:TPU:64 now
where the time goes in v1:
time: 154 us; the launch traced here: 153 us
  starting transfers between devices  51.1 us (33%)
  Pallas kernels  44.5 us (29%)
  waiting for transfers between devices  44 us (29%)
  local copies, waits for them, and re-layouts  10.5 us (7%)
  other arithmetic  2.14 us (1%)
    ppermute x4, starting transfers between devices, body(): zs.append(lax.ppermute(zs[-1], 'ctx', Z_STEP))  18.2 us
    ppermute x3, waiting for transfers between devices, body(): lax.ppermute(jnp.concatenate([edge, zs[1], zs[2], zs[3]], axis=0), 'ctx',...  17.1 us
    pallas_call x1, Pallas kernels, body(): pl.pallas_call(attend_kernel, in_specs=smem(2) + vmem(9), out_specs=pl.Bl...  16.5 us
    ppermute x3, waiting for transfers between devices, body(): carry = lax.ppermute(carry, 'ctx', Z_STEP)  15.5 us
    pallas_call x1, Pallas kernels, body(): pl.pallas_call(project_kernel, grid_spec=pltpu.PrefetchScalarGridSpec(num...  9.47 us
    ppermute x3, starting transfers between devices, body(): lax.ppermute(summed[k].astype(BF16), 'tp', y_shift(k)).astype(F32)  7.56 us
    ppermute x3, starting transfers between devices, body(): carry = lax.ppermute(carry, 'ctx', Z_STEP)  7.53 us
    ppermute x4, waiting for transfers between devices, body(): zs.append(lax.ppermute(zs[-1], 'ctx', Z_STEP))  5.79 us
  transfers between devices with their start and end apart: 21, of which 7 were waited for; matrix products, arithmetic and copies ran while one was open for 4% of the time, Pallas kernels for 29%

profile of v1, /device:TPU:64, one launch (start us, length us, event | category | flops | bytes accessed | tf_op | source)
XLA Modules:
  0.0 153.3 jit_solution(14151610887173025073)
XLA Ops:
  0.6 0.9 constant_dynamic-update-slice_fusion.1
  1.5 0.9 constant_dynamic-update-slice_fusion.own
  2.4 3.8 %collective-permute-start.10 = (bf16[256,256]{1,0:T(8,128)(2,1)S(1)}, bf16[256,256]{1,0:T(8,128)(2,1)S(1)}, u32[]{:S(2)}, u32[]{:S(2)}) collective-permute-start(bf16[256,256]{1,0:T(8,128)(2,1)S(1)} %constant_dynamic-update-slice_fusion.own), channel_id=1, source_target_pairs={{0,32},{8,40},{16,48},{24,56},{32,64},{40,72},{48,80},{56,88},{64,... | collective-permute-start | bytes 393224 | tf_op jit(solution)/shard_map/ppermute | solution.py:297
  6.2 3.3 %collective-permute-done.10.z1 = bf16[256,256]{1,0:T(8,128)(2,1)S(1)} collective-permute-done((bf16[256,256]{1,0:T(8,128)(2,1)S(1)}, bf16[256,256]{1,0:T(8,128)(2,1)S(1)}, u32[]{:S(2)}, u32[]{:S(2)}) %collective-permute-start.10) | collective-permute-done | bytes 131104 | tf_op jit(solution)/shard_map/ppermute | solution.py:297
  9.5 4.5 %collective-permute-start.11 = (bf16[256,256]{1,0:T(8,128)(2,1)S(1)}, bf16[256,256]{1,0:T(8,128)(2,1)S(1)}, u32[]{:S(2)}, u32[]{:S(2)}) collective-permute-start(bf16[256,256]{1,0:T(8,128)(2,1)S(1)} %collective-permute-done.10.z1), channel_id=1, source_target_pairs={{0,32},{8,40},{16,48},{24,56},{32,64},{40,72},{48,80},{56,88},{64,... | collective-permute-start | bytes 393224 | tf_op jit(solution)/shard_map/ppermute | solution.py:297
  14.0 1.3 copy.16.bias_ref
  15.3 1.3 copy.17.alog_ref
  16.7 0.7 pad_add_fusion.place
  17.3 4.1 %chunk_states.1 = (bf16[272,512]{1,0:T(8,128)(2,1)}, bf16[272,512]{1,0:T(8,128)(2,1)}, bf16[272,512]{1,0:T(8,128)(2,1)}, bf16[272,512]{1,0:T(8,128)(2,1)}, f32[3...) custom-call(s32[4]{0:T(128)} %pad_add_fusion.place, s32[4]{0:T(128)} %lengths.5, bf16[256,2048]{1,0:T(8,128)(2,1)} %x_ref.3, ...), custom_call_target="tpu_custom_call" | custom-call | tf_op jit(solution)/shard_map/chunk_states/pallas_call | solution.py:299
  21.5 1.5 collective-permute-start
  23.0 2.7 %collective-permute-start.1 = (bf16[272,512]{1,0:T(8,128)(2,1)}, bf16[272,512]{1,0:T(8,128)(2,1)S(1)}, u32[]{:S(2)}, u32[]{:S(2)}) collective-permute-start(bf16[272,512]{1,0:T(8,128)(2,1)} %get-tuple-element.22), channel_id=1, source_target_pairs={{0,16},{8,24},{16,0},{24,8},{32,48},{40,56},{48,32},{56,40},{64,80... | collective-permute-start | bytes 835592 | tf_op jit(solution)/shard_map/ppermute | solution.py:308
  25.7 1.4 collective-permute-start.2
  27.1 5.6 %collective-permute-start.12 = (bf16[256,256]{1,0:T(8,128)(2,1)S(1)}, bf16[256,256]{1,0:T(8,128)(2,1)S(1)}, u32[]{:S(2)}, u32[]{:S(2)}) collective-permute-start(bf16[256,256]{1,0:T(8,128)(2,1)S(1)} %collective-permute-done.11.z2), channel_id=1, source_target_pairs={{0,32},{8,40},{16,48},{24,56},{32,64},{40,72},{48,80},{56,88},{64,... | collective-permute-start | bytes 393224 | tf_op jit(solution)/shard_map/ppermute | solution.py:297
  32.7 2.5 %collective-permute-done.12.z3 = bf16[256,256]{1,0:T(8,128)(2,1)S(1)} collective-permute-done((bf16[256,256]{1,0:T(8,128)(2,1)S(1)}, bf16[256,256]{1,0:T(8,128)(2,1)S(1)}, u32[]{:S(2)}, u32[]{:S(2)}) %collective-permute-start.12) | collective-permute-done | bytes 131104 | tf_op jit(solution)/shard_map/ppermute | solution.py:297
  35.2 4.3 %collective-permute-start.13 = (bf16[256,256]{1,0:T(8,128)(2,1)S(1)}, bf16[256,256]{1,0:T(8,128)(2,1)S(1)}, u32[]{:S(2)}, u32[]{:S(2)}) collective-permute-start(bf16[256,256]{1,0:T(8,128)(2,1)S(1)} %collective-permute-done.12.z3), channel_id=1, source_target_pairs={{0,32},{8,40},{16,48},{24,56},{32,64},{40,72},{48,80},{56,88},{64,... | collective-permute-start | bytes 393224 | tf_op jit(solution)/shard_map/ppermute | solution.py:297
  39.6 0.0 collective-permute-done.a1
  39.6 0.0 collective-permute-done.1.a2
  39.6 0.7 copy-done.10
  40.3 0.1 copy-done.11
  40.4 0.1 copy-done.12
  40.5 2.7 %row_scan.1 = (bf16[4,256,512]{2,1,0:T(8,128)(2,1)}, bf16[256,512]{1,0:T(8,128)(2,1)}, f32[4,8,512]{2,1,0:T(8,128)}, f32[8,512]{1,0:T(8,128)}) custom-call(s32[4]{0:T(128)} %pad_add_fusion.place, bf16[272,512]{1,0:T(8,128)(2,1)} %get-tuple-element.20.a0, bf16[272,512]{1,0:T(8,128)(2,1)} %copy-done.10, bf16[272,512]{1,0:T(8,128)(2,1)} %copy-done.11, ...), custom_call_target="tpu_custom_call" | custom-call | tf_op jit(solution)/shard_map/row_scan/pallas_call | solution.py:309
  43.3 3.3 %collective-permute-start.3 = (bf16[256,512]{1,0:T(8,128)(2,1)}, bf16[256,512]{1,0:T(8,128)(2,1)S(1)}, u32[]{:S(2)}, u32[]{:S(2)}) collective-permute-start(bf16[256,512]{1,0:T(8,128)(2,1)} %get-tuple-element.26), channel_id=1, source_target_pairs={{0,32},{8,40},{16,48},{24,56},{32,64},{40,72},{48,80},{56,88},{64,... | collective-permute-start | bytes 786440 | tf_op jit(solution)/shard_map/ppermute | solution.py:324
  46.6 0.1 pad_maximum_fusion
  46.7 1.2 collective-permute-start.14
  47.9 2.4 %collective-permute-start.15 = (bf16[1024,256]{1,0:T(8,128)(2,1)S(1)}, bf16[1024,256]{1,0:T(8,128)(2,1)S(1)}, u32[]{:S(2)}, u32[]{:S(2)}) collective-permute-start(bf16[1024,256]{1,0:T(8,128)(2,1)S(1)} %get-tuple-element.36), channel_id=1, source_target_pairs={{0,16},{8,24},{16,0},{24,8},{32,48},{40,56},{48,32},{56,40},{64,80... | collective-permute-start | bytes 1572872 | tf_op jit(solution)/shard_map/ppermute | solution.py:322
  50.3 1.6 %collective-permute-start.16 = (bf16[1024,256]{1,0:T(8,128)(2,1)S(1)}, bf16[1024,256]{1,0:T(8,128)(2,1)S(1)}, u32[]{:S(2)}, u32[]{:S(2)}) collective-permute-start(bf16[1024,256]{1,0:T(8,128)(2,1)S(1)} %get-tuple-element.35), channel_id=1, source_target_pairs={{0,24},{8,0},{16,8},{24,16},{32,56},{40,32},{48,40},{56,48},{64,88... | collective-permute-start | bytes 1572872 | tf_op jit(solution)/shard_map/ppermute | solution.py:322
  51.8 0.7 slice.32
  52.6 0.0 collective-permute-done.3
  52.6 0.1 fusion
  52.7 2.6 %collective-permute-start.4 = (bf16[256,512]{1,0:T(8,128)(2,1)S(1)}, bf16[256,512]{1,0:T(8,128)(2,1)S(1)}, u32[]{:S(2)}, u32[]{:S(2)}) collective-permute-start(bf16[256,512]{1,0:T(8,128)(2,1)S(1)} %fusion), channel_id=1, source_target_pairs={{0,32},{8,40},{16,48},{24,56},{32,64},{40,72},{48,80},{56,88},{64,... | collective-permute-start | bytes 786440 | tf_op jit(solution)/shard_map/ppermute | solution.py:327
  55.3 5.5 %collective-permute-done.14.g1 = bf16[1024,256]{1,0:T(8,128)(2,1)S(1)} collective-permute-done((bf16[1024,256]{1,0:T(8,128)(2,1)S(1)}, bf16[1024,256]{1,0:T(8,128)(2,1)S(1)}, u32[]{:S(2)}, u32[]{:S(2)}) %collective-permute-start.14) | collective-permute-done | bytes 524320 | tf_op jit(solution)/shard_map/ppermute | solution.py:322
  60.8 11.6 %collective-permute-done.15.g2 = bf16[1024,256]{1,0:T(8,128)(2,1)S(1)} collective-permute-done((bf16[1024,256]{1,0:T(8,128)(2,1)S(1)}, bf16[1024,256]{1,0:T(8,128)(2,1)S(1)}, u32[]{:S(2)}, u32[]{:S(2)}) %collective-permute-start.15) | collective-permute-done | bytes 524320 | tf_op jit(solution)/shard_map/ppermute | solution.py:322
  72.4 0.0 collective-permute-done.16.g3
  72.4 0.8 copy-done.8
  73.2 0.8 copy-done.9
  74.0 16.5 %attend.1.a_ref = bf16[8,256,128]{2,1,0:T(8,128)(2,1)} custom-call(s32[4]{0:T(128)} %pad_add_fusion.place, s32[4]{0:T(128)} %lengths.5, bf16[256,1024]{1,0:T(8,128)(2,1)} %q_ref.1, bf16[256,256]{1,0:T(8,128)(2,1)} %copy-done.2, bf16[256,256]{1,0:T(8,128)(2,1)} %copy-done.3, bf16[256,256]{1,0:T(8,128)(2,1)} %copy-done.4, bf16[256,256]{1,0:T(8,128)(2,1)} %copy-done.5, ...), custom_call_target="tpu_custom_call" | custom-call | tf_op jit(solution)/shard_map/attend/pallas_call | solution.py:349
  90.5 9.5 %project.1 = bf16[8,256,512]{2,1,0:T(8,128)(2,1)} custom-call(s32[4]{0:T(128)} %pad_add_fusion.place, bf16[8,256,128]{2,1,0:T(8,128)(2,1)} %attend.1.a_ref, bf16[1024,4096]{1,0:T(8,128)(2,1)} %w_ref.1), custom_call_target="tpu_custom_call" | custom-call | tf_op jit(solution)/shard_map/project/pallas_call | solution.py:372
  100.0 1.4 slice.43
  101.5 0.1 collective-permute-start.17
  101.6 0.0 collective-permute-done.4
  101.6 0.1 fusion.1
  101.7 2.5 %collective-permute-start.5 = (bf16[256,512]{1,0:T(8,128)(2,1)S(1)}, bf16[256,512]{1,0:T(8,128)(2,1)S(1)}, u32[]{:S(2)}, u32[]{:S(2)}) collective-permute-start(bf16[256,512]{1,0:T(8,128)(2,1)S(1)} %fusion.1), channel_id=1, source_target_pairs={{0,32},{8,40},{16,48},{24,56},{32,64},{40,72},{48,80},{56,88},{64,... | collective-permute-start | bytes 786440 | tf_op jit(solution)/shard_map/ppermute | solution.py:327
  104.1 8.1 %collective-permute-done.5 = bf16[256,512]{1,0:T(8,128)(2,1)S(1)} collective-permute-done((bf16[256,512]{1,0:T(8,128)(2,1)S(1)}, bf16[256,512]{1,0:T(8,128)(2,1)S(1)}, u32[]{:S(2)}, u32[]{:S(2)}) %collective-permute-start.5) | collective-permute-done | bytes 262176 | tf_op jit(solution)/shard_map/ppermute | solution.py:327
  112.3 0.1 fusion.2
  112.3 2.5 %collective-permute-start.6 = (bf16[256,512]{1,0:T(8,128)(2,1)S(1)}, bf16[256,512]{1,0:T(8,128)(2,1)S(1)}, u32[]{:S(2)}, u32[]{:S(2)}) collective-permute-start(bf16[256,512]{1,0:T(8,128)(2,1)S(1)} %fusion.2), channel_id=1, source_target_pairs={{0,32},{8,40},{16,48},{24,56},{32,64},{40,72},{48,80},{56,88},{64,... | collective-permute-start | bytes 786440 | tf_op jit(solution)/shard_map/ppermute | solution.py:327
  114.8 7.3 %collective-permute-done.6.r_ref = bf16[256,512]{1,0:T(8,128)(2,1)S(1)} collective-permute-done((bf16[256,512]{1,0:T(8,128)(2,1)S(1)}, bf16[256,512]{1,0:T(8,128)(2,1)S(1)}, u32[]{:S(2)}, u32[]{:S(2)}) %collective-permute-start.6) | collective-permute-done | bytes 262176 | tf_op jit(solution)/shard_map/ppermute | solution.py:327
  122.1 0.7 copy-done.16
  122.8 2.4 %row_states.1 = (bf16[256,512]{1,0:T(8,128)(2,1)}, bf16[256,512]{1,0:T(8,128)(2,1)}, bf16[256,512]{1,0:T(8,128)(2,1)}, bf16[256,512]{1,0:T(8,128)(2,1)}) custom-call(s32[4]{0:T(128)} %pad_add_fusion.place, bf16[4,256,512]{2,1,0:T(8,128)(2,1)} %get-tuple-element.24.p_ref, f32[4,8,512]{2,1,0:T(8,128)} %get-tuple-element.25.pth_ref, bf16[256,512]{1,0:T(8,128)(2,1)} %copy-done.16), custom_call_target="tpu_custom_call" | custom-call | tf_op jit(solution)/shard_map/row_states/pallas_call | solution.py:328
  125.3 0.3 collective-permute-start.7
  125.6 2.5 %collective-permute-start.8 = (bf16[256,512]{1,0:T(8,128)(2,1)}, bf16[256,512]{1,0:T(8,128)(2,1)S(1)}, u32[]{:S(2)}, u32[]{:S(2)}) collective-permute-start(bf16[256,512]{1,0:T(8,128)(2,1)} %get-tuple-element.30), channel_id=1, source_target_pairs={{0,16},{8,24},{16,0},{24,8},{32,48},{40,56},{48,32},{56,40},{64,80... | collective-permute-start | bytes 786440 | tf_op jit(solution)/shard_map/ppermute | solution.py:336
  128.1 0.9 collective-permute-start.9
  128.9 0.0 collective-permute-done.17
  128.9 0.2 fusion.6
  129.2 1.7 %collective-permute-start.18 = (bf16[256,512]{1,0:T(8,128)(2,1)S(1)}, bf16[256,512]{1,0:T(8,128)(2,1)S(1)}, u32[]{:S(2)}, u32[]{:S(2)}) collective-permute-start(bf16[256,512]{1,0:T(8,128)(2,1)S(1)} %get-tuple-element.32), channel_id=1, source_target_pairs={{0,2},{1,3},{2,4},{3,5},{4,6},{5,7},{6,0},{7,1},{8,10},{9,11},{10,... | collective-permute-start | bytes 786440 | tf_op jit(solution)/shard_map/ppermute | solution.py:392
  130.8 2.9 %collective-permute-start.19 = (bf16[256,512]{1,0:T(8,128)(2,1)S(1)}, bf16[256,512]{1,0:T(8,128)(2,1)S(1)}, u32[]{:S(2)}, u32[]{:S(2)}) collective-permute-start(bf16[256,512]{1,0:T(8,128)(2,1)S(1)} %get-tuple-element.34), channel_id=1, source_target_pairs={{0,4},{1,5},{2,6},{3,7},{4,0},{5,1},{6,2},{7,3},{8,12},{9,13},{10,... | collective-permute-start | bytes 786440 | tf_op jit(solution)/shard_map/ppermute | solution.py:392
  133.7 5.6 %collective-permute-done.7.i1 = bf16[256,512]{1,0:T(8,128)(2,1)S(1)} collective-permute-done((bf16[256,512]{1,0:T(8,128)(2,1)}, bf16[256,512]{1,0:T(8,128)(2,1)S(1)}, u32[]{:S(2)}, u32[]{:S(2)}) %collective-permute-start.7) | collective-permute-done | bytes 262176 | tf_op jit(solution)/shard_map/ppermute | solution.py:336
  139.3 3.0 %collective-permute-start.20 = (bf16[256,512]{1,0:T(8,128)(2,1)S(1)}, bf16[256,512]{1,0:T(8,128)(2,1)S(1)}, u32[]{:S(2)}, u32[]{:S(2)}) collective-permute-start(bf16[256,512]{1,0:T(8,128)(2,1)S(1)} %get-tuple-element.33), channel_id=1, source_target_pairs={{0,6},{1,7},{2,0},{3,1},{4,2},{5,3},{6,4},{7,5},{8,14},{9,15},{10,... | collective-permute-start | bytes 786440 | tf_op jit(solution)/shard_map/ppermute | solution.py:392
  142.3 4.5 %within_chunk.1.y_ref = f32[256,2048]{1,0:T(8,128)} custom-call(s32[4]{0:T(128)} %pad_add_fusion.place, s32[4]{0:T(128)} %lengths.5, bf16[256,2048]{1,0:T(8,128)(2,1)} %x_ref.3, bf16[256,256]{1,0:T(8,128)(2,1)} %b_ref.3, bf16[256,256]{1,0:T(8,128)(2,1)} %c_ref.3, f32[32,256]{1,0:T(8,128)} %get-tuple-element.17.d_ref, f32[256,32]{1,0:T(8,128)} %get-tuple-element.18.cumt_ref, ...), custom_call_target="tpu_custom_call" | custom-call | tf_op jit(solution)/shard_map/within_chunk/pallas_call | solution.py:338
  146.9 0.0 collective-permute-done.8.i2
  146.9 0.7 copy-done.14
  147.6 0.1 copy-done.15
  147.7 4.7 %carry_gate_norm.1 = bf16[256,2048]{1,0:T(8,128)(2,1)} custom-call(s32[4]{0:T(128)} %pad_add_fusion.place, f32[256,2048]{1,0:T(8,128)} %within_chunk.1.y_ref, bf16[256,256]{1,0:T(8,128)(2,1)} %c_ref.3, f32[256,32]{1,0:T(8,128)} %get-tuple-element.19.lead_ref, bf16[256,2048]{1,0:T(8,128)(2,1)} %gate_ref.1, f32[1,2048]{1,0:T(1,128)} %bitcast.26, ...), custom_call_target="tpu_custom_call" | custom-call | tf_op jit(solution)/shard_map/carry_gate_norm/pallas_call | solution.py:395
  152.4 0.0 collective-permute-done.18
  152.4 0.9 fusion.5
  (33 shorter events, 0.1 us)
Async XLA Ops:
  2.3 44.4 %copy-start.2 = (bf16[256,256]{1,0:T(8,128)(2,1)}, bf16[256,256]{1,0:T(8,128)(2,1)S(1)}, u32[]{:S(2)}) copy-start(bf16[256,256]{1,0:T(8,128)(2,1)S(1)} %constant_dynamic-update-slice_fusion.own) | copy-start | bytes 393220
  2.4 7.1 %collective-permute-start.10 = (bf16[256,256]{1,0:T(8,128)(2,1)S(1)}, bf16[256,256]{1,0:T(8,128)(2,1)S(1)}, u32[]{:S(2)}, u32[]{:S(2)}) collective-permute-start(bf16[256,256]{1,0:T(8,128)(2,1)S(1)} %constant_dynamic-update-slice_fusion.own), channel_id=1, source_target_pairs={{0,32},{8,40},{16,48},{24,56},{32,64},{40,72},{48,80},{56,88},{64,... | collective-permute-start | bytes 393224 | tf_op jit(solution)/shard_map/ppermute | solution.py:297
  9.5 37.2 %copy-start.3 = (bf16[256,256]{1,0:T(8,128)(2,1)}, bf16[256,256]{1,0:T(8,128)(2,1)S(1)}, u32[]{:S(2)}) copy-start(bf16[256,256]{1,0:T(8,128)(2,1)S(1)} %collective-permute-done.10.z1) | copy-start | bytes 393220
  9.5 17.6 %collective-permute-start.11 = (bf16[256,256]{1,0:T(8,128)(2,1)S(1)}, bf16[256,256]{1,0:T(8,128)(2,1)S(1)}, u32[]{:S(2)}, u32[]{:S(2)}) collective-permute-start(bf16[256,256]{1,0:T(8,128)(2,1)S(1)} %collective-permute-done.10.z1), channel_id=1, source_target_pairs={{0,32},{8,40},{16,48},{24,56},{32,64},{40,72},{48,80},{56,88},{64,... | collective-permute-start | bytes 393224 | tf_op jit(solution)/shard_map/ppermute | solution.py:297
  21.5 18.1 %collective-permute-start = (bf16[272,512]{1,0:T(8,128)(2,1)}, bf16[272,512]{1,0:T(8,128)(2,1)S(1)}, u32[]{:S(2)}, u32[]{:S(2)}) collective-permute-start(bf16[272,512]{1,0:T(8,128)(2,1)} %get-tuple-element.21), channel_id=1, source_target_pairs={{0,8},{8,16},{16,24},{24,0},{32,40},{40,48},{48,56},{56,32},{64,72... | collective-permute-start | bytes 835592 | tf_op jit(solution)/shard_map/ppermute | solution.py:308
  23.0 16.7 %collective-permute-start.1 = (bf16[272,512]{1,0:T(8,128)(2,1)}, bf16[272,512]{1,0:T(8,128)(2,1)S(1)}, u32[]{:S(2)}, u32[]{:S(2)}) collective-permute-start(bf16[272,512]{1,0:T(8,128)(2,1)} %get-tuple-element.22), channel_id=1, source_target_pairs={{0,16},{8,24},{16,0},{24,8},{32,48},{40,56},{48,32},{56,40},{64,80... | collective-permute-start | bytes 835592 | tf_op jit(solution)/shard_map/ppermute | solution.py:308
  25.7 13.9 %collective-permute-start.2 = (bf16[272,512]{1,0:T(8,128)(2,1)}, bf16[272,512]{1,0:T(8,128)(2,1)S(1)}, u32[]{:S(2)}, u32[]{:S(2)}) collective-permute-start(bf16[272,512]{1,0:T(8,128)(2,1)} %get-tuple-element.23), channel_id=1, source_target_pairs={{0,24},{8,0},{16,8},{24,16},{32,56},{40,32},{48,40},{56,48},{64,88... | collective-permute-start | bytes 835592 | tf_op jit(solution)/shard_map/ppermute | solution.py:308
  27.1 25.5 %copy-start.4 = (bf16[256,256]{1,0:T(8,128)(2,1)}, bf16[256,256]{1,0:T(8,128)(2,1)S(1)}, u32[]{:S(2)}) copy-start(bf16[256,256]{1,0:T(8,128)(2,1)S(1)} %collective-permute-done.11.z2) | copy-start | bytes 393220
  27.1 8.1 %collective-permute-start.12 = (bf16[256,256]{1,0:T(8,128)(2,1)S(1)}, bf16[256,256]{1,0:T(8,128)(2,1)S(1)}, u32[]{:S(2)}, u32[]{:S(2)}) collective-permute-start(bf16[256,256]{1,0:T(8,128)(2,1)S(1)} %collective-permute-done.11.z2), channel_id=1, source_target_pairs={{0,32},{8,40},{16,48},{24,56},{32,64},{40,72},{48,80},{56,88},{64,... | collective-permute-start | bytes 393224 | tf_op jit(solution)/shard_map/ppermute | solution.py:297
  35.2 17.4 %copy-start.5 = (bf16[256,256]{1,0:T(8,128)(2,1)}, bf16[256,256]{1,0:T(8,128)(2,1)S(1)}, u32[]{:S(2)}) copy-start(bf16[256,256]{1,0:T(8,128)(2,1)S(1)} %collective-permute-done.12.z3) | copy-start | bytes 393220
  35.2 11.3 %collective-permute-start.13 = (bf16[256,256]{1,0:T(8,128)(2,1)S(1)}, bf16[256,256]{1,0:T(8,128)(2,1)S(1)}, u32[]{:S(2)}, u32[]{:S(2)}) collective-permute-start(bf16[256,256]{1,0:T(8,128)(2,1)S(1)} %collective-permute-done.12.z3), channel_id=1, source_target_pairs={{0,32},{8,40},{16,48},{24,56},{32,64},{40,72},{48,80},{56,88},{64,... | collective-permute-start | bytes 393224 | tf_op jit(solution)/shard_map/ppermute | solution.py:297
  39.6 0.7 copy-start.10
  39.6 0.8 copy-start.11
  39.6 0.9 copy-start.12
  43.3 9.3 %copy-start.1 = (bf16[256,512]{1,0:T(8,128)(2,1)S(1)}, bf16[256,512]{1,0:T(8,128)(2,1)}, u32[]{:S(2)}) copy-start(bf16[256,512]{1,0:T(8,128)(2,1)} %get-tuple-element.26) | copy-start | bytes 786436
  43.3 9.3 %collective-permute-start.3 = (bf16[256,512]{1,0:T(8,128)(2,1)}, bf16[256,512]{1,0:T(8,128)(2,1)S(1)}, u32[]{:S(2)}, u32[]{:S(2)}) collective-permute-start(bf16[256,512]{1,0:T(8,128)(2,1)} %get-tuple-element.26), channel_id=1, source_target_pairs={{0,32},{8,40},{16,48},{24,56},{32,64},{40,72},{48,80},{56,88},{64,... | collective-permute-start | bytes 786440 | tf_op jit(solution)/shard_map/ppermute | solution.py:324
  46.5 25.9 %copy-start.6 = (bf16[256,256]{1,0:T(8,128)(2,1)}, bf16[256,256]{1,0:T(8,128)(2,1)S(1)}, u32[]{:S(2)}) copy-start(bf16[256,256]{1,0:T(8,128)(2,1)S(1)} %collective-permute-done.13.z4) | copy-start | bytes 393220
  46.7 14.0 %collective-permute-start.14 = (bf16[1024,256]{1,0:T(8,128)(2,1)S(1)}, bf16[1024,256]{1,0:T(8,128)(2,1)S(1)}, u32[]{:S(2)}, u32[]{:S(2)}) collective-permute-start(bf16[1024,256]{1,0:T(8,128)(2,1)S(1)} %get-tuple-element.37), channel_id=1, source_target_pairs={{0,8},{8,16},{16,24},{24,0},{32,40},{40,48},{48,56},{56,32},{64,72... | collective-permute-start | bytes 1572872 | tf_op jit(solution)/shard_map/ppermute | solution.py:322
  47.9 24.5 %collective-permute-start.15 = (bf16[1024,256]{1,0:T(8,128)(2,1)S(1)}, bf16[1024,256]{1,0:T(8,128)(2,1)S(1)}, u32[]{:S(2)}, u32[]{:S(2)}) collective-permute-start(bf16[1024,256]{1,0:T(8,128)(2,1)S(1)} %get-tuple-element.36), channel_id=1, source_target_pairs={{0,16},{8,24},{16,0},{24,8},{32,48},{40,56},{48,32},{56,40},{64,80... | collective-permute-start | bytes 1572872 | tf_op jit(solution)/shard_map/ppermute | solution.py:322
  50.3 22.1 %collective-permute-start.16 = (bf16[1024,256]{1,0:T(8,128)(2,1)S(1)}, bf16[1024,256]{1,0:T(8,128)(2,1)S(1)}, u32[]{:S(2)}, u32[]{:S(2)}) collective-permute-start(bf16[1024,256]{1,0:T(8,128)(2,1)S(1)} %get-tuple-element.35), channel_id=1, source_target_pairs={{0,24},{8,0},{16,8},{24,16},{32,56},{40,32},{48,40},{56,48},{64,88... | collective-permute-start | bytes 1572872 | tf_op jit(solution)/shard_map/ppermute | solution.py:322
  52.7 48.9 %collective-permute-start.4 = (bf16[256,512]{1,0:T(8,128)(2,1)S(1)}, bf16[256,512]{1,0:T(8,128)(2,1)S(1)}, u32[]{:S(2)}, u32[]{:S(2)}) collective-permute-start(bf16[256,512]{1,0:T(8,128)(2,1)S(1)} %fusion), channel_id=1, source_target_pairs={{0,32},{8,40},{16,48},{24,56},{32,64},{40,72},{48,80},{56,88},{64,... | collective-permute-start | bytes 786440 | tf_op jit(solution)/shard_map/ppermute | solution.py:327
  60.8 11.7 %copy-start.7 = (bf16[1024,256]{1,0:T(8,128)(2,1)}, bf16[1024,256]{1,0:T(8,128)(2,1)S(1)}, u32[]{:S(2)}) copy-start(bf16[1024,256]{1,0:T(8,128)(2,1)S(1)} %collective-permute-done.14.g1) | copy-start | bytes 1572868
  72.4 0.8 copy-start.8
  73.2 0.8 copy-start.9
  100.0 28.9 %copy-start = (bf16[8,256,512]{2,1,0:T(8,128)(2,1)S(1)}, bf16[8,256,512]{2,1,0:T(8,128)(2,1)}, u32[]{:S(2)}) copy-start(bf16[8,256,512]{2,1,0:T(8,128)(2,1)} %project.1) | copy-start | bytes 6291460
  101.5 27.5 %collective-permute-start.17 = (bf16[4,256,512]{2,1,0:T(8,128)(2,1)S(1)}, bf16[4,256,512]{2,1,0:T(8,128)(2,1)S(1)}, u32[]{:S(2)}, u32[]{:S(2)}) collective-permute-start(bf16[4,256,512]{2,1,0:T(8,128)(2,1)S(1)} %slice.43), channel_id=1, source_target_pairs={{0,1},{1,0},{2,3},{3,2},{4,5},{5,4},{6,7},{7,6},{8,9},{9,8},{10,11... | collective-permute-start | bytes 3145736 | tf_op jit(solution)/shard_map/ppermute | solution.py:388
  101.7 10.6 %collective-permute-start.5 = (bf16[256,512]{1,0:T(8,128)(2,1)S(1)}, bf16[256,512]{1,0:T(8,128)(2,1)S(1)}, u32[]{:S(2)}, u32[]{:S(2)}) collective-permute-start(bf16[256,512]{1,0:T(8,128)(2,1)S(1)} %fusion.1), channel_id=1, source_target_pairs={{0,32},{8,40},{16,48},{24,56},{32,64},{40,72},{48,80},{56,88},{64,... | collective-permute-start | bytes 786440 | tf_op jit(solution)/shard_map/ppermute | solution.py:327
  112.3 9.8 %collective-permute-start.6 = (bf16[256,512]{1,0:T(8,128)(2,1)S(1)}, bf16[256,512]{1,0:T(8,128)(2,1)S(1)}, u32[]{:S(2)}, u32[]{:S(2)}) collective-permute-start(bf16[256,512]{1,0:T(8,128)(2,1)S(1)} %fusion.2), channel_id=1, source_target_pairs={{0,32},{8,40},{16,48},{24,56},{32,64},{40,72},{48,80},{56,88},{64,... | collective-permute-start | bytes 786440 | tf_op jit(solution)/shard_map/ppermute | solution.py:327
  122.1 0.7 copy-start.16
  125.3 14.1 %collective-permute-start.7 = (bf16[256,512]{1,0:T(8,128)(2,1)}, bf16[256,512]{1,0:T(8,128)(2,1)S(1)}, u32[]{:S(2)}, u32[]{:S(2)}) collective-permute-start(bf16[256,512]{1,0:T(8,128)(2,1)} %get-tuple-element.29), channel_id=1, source_target_pairs={{0,8},{8,16},{16,24},{24,0},{32,40},{40,48},{48,56},{56,32},{64,72... | collective-permute-start | bytes 786440 | tf_op jit(solution)/shard_map/ppermute | solution.py:336
  125.6 21.3 %collective-permute-start.8 = (bf16[256,512]{1,0:T(8,128)(2,1)}, bf16[256,512]{1,0:T(8,128)(2,1)S(1)}, u32[]{:S(2)}, u32[]{:S(2)}) collective-permute-start(bf16[256,512]{1,0:T(8,128)(2,1)} %get-tuple-element.30), channel_id=1, source_target_pairs={{0,16},{8,24},{16,0},{24,8},{32,48},{40,56},{48,32},{56,40},{64,80... | collective-permute-start | bytes 786440 | tf_op jit(solution)/shard_map/ppermute | solution.py:336
  128.1 18.8 %collective-permute-start.9 = (bf16[256,512]{1,0:T(8,128)(2,1)}, bf16[256,512]{1,0:T(8,128)(2,1)S(1)}, u32[]{:S(2)}, u32[]{:S(2)}) collective-permute-start(bf16[256,512]{1,0:T(8,128)(2,1)} %get-tuple-element.31), channel_id=1, source_target_pairs={{0,24},{8,0},{16,8},{24,16},{32,56},{40,32},{48,40},{56,48},{64,88... | collective-permute-start | bytes 786440 | tf_op jit(solution)/shard_map/ppermute | solution.py:336
  129.2 23.2 %collective-permute-start.18 = (bf16[256,512]{1,0:T(8,128)(2,1)S(1)}, bf16[256,512]{1,0:T(8,128)(2,1)S(1)}, u32[]{:S(2)}, u32[]{:S(2)}) collective-permute-start(bf16[256,512]{1,0:T(8,128)(2,1)S(1)} %get-tuple-element.32), channel_id=1, source_target_pairs={{0,2},{1,3},{2,4},{3,5},{4,6},{5,7},{6,0},{7,1},{8,10},{9,11},{10,... | collective-permute-start | bytes 786440 | tf_op jit(solution)/shard_map/ppermute | solution.py:392
  130.8 21.6 %collective-permute-start.19 = (bf16[256,512]{1,0:T(8,128)(2,1)S(1)}, bf16[256,512]{1,0:T(8,128)(2,1)S(1)}, u32[]{:S(2)}, u32[]{:S(2)}) collective-permute-start(bf16[256,512]{1,0:T(8,128)(2,1)S(1)} %get-tuple-element.34), channel_id=1, source_target_pairs={{0,4},{1,5},{2,6},{3,7},{4,0},{5,1},{6,2},{7,3},{8,12},{9,13},{10,... | collective-permute-start | bytes 786440 | tf_op jit(solution)/shard_map/ppermute | solution.py:392
  139.3 7.6 %copy-start.13 = (bf16[256,512]{1,0:T(8,128)(2,1)}, bf16[256,512]{1,0:T(8,128)(2,1)S(1)}, u32[]{:S(2)}) copy-start(bf16[256,512]{1,0:T(8,128)(2,1)S(1)} %collective-permute-done.7.i1) | copy-start | bytes 786436
  139.3 13.1 %collective-permute-start.20 = (bf16[256,512]{1,0:T(8,128)(2,1)S(1)}, bf16[256,512]{1,0:T(8,128)(2,1)S(1)}, u32[]{:S(2)}, u32[]{:S(2)}) collective-permute-start(bf16[256,512]{1,0:T(8,128)(2,1)S(1)} %get-tuple-element.33), channel_id=1, source_target_pairs={{0,6},{1,7},{2,0},{3,1},{4,2},{5,3},{6,4},{7,5},{8,14},{9,15},{10,... | collective-permute-start | bytes 786440 | tf_op jit(solution)/shard_map/ppermute | solution.py:392
  146.9 0.7 copy-start.14
  146.9 0.8 copy-start.15

commit v2 on v1

v2 whole, which is shorter than its diff:
```python
import math

import jax
import jax.numpy as jnp
from jax import lax
from jax.experimental import pallas as pl
from jax.experimental.pallas import tpu as pltpu
from jax.sharding import PartitionSpec as P

HEAD_P = 64
STATE = 256
HEAD_DIM = 128
NZ = 8
NX = 4
NY = 4
LOG2E = math.log2(math.e)
EPS = 1e-05
BIG = -1e30
F32 = jnp.float32
BF16 = jnp.bfloat16
EXTRA = 16
QUARTER = 512


def iota(shape, dim):
    return lax.broadcasted_iota(jnp.int32, shape, dim)


def split3(a):
    hi = a.astype(BF16)
    rest = a - hi.astype(F32)
    mid = rest.astype(BF16)
    low = (rest - mid.astype(F32)).astype(BF16)
    return hi, mid, low


def spread(a, expand, terms=3):
    total = None
    for part in split3(a)[:terms]:
        one = jnp.dot(part, expand, preferred_element_type=F32)
        total = one if total is None else total + one
    return total


def expander(heads, lanes):
    return (iota((heads, lanes), 1) // HEAD_P == iota((heads, lanes), 0)).astype(F32).astype(BF16)


def place_of():
    ctx = lax.axis_index("ctx")
    return ctx // NX, lax.rem(ctx, NX)


def ends_of(lengths):
    e0 = lengths[0]
    e1 = e0 + lengths[1]
    e2 = e1 + lengths[2]
    return e0, e1, e2, e2 + lengths[3]


def rollout_at(pos, ends):
    count = jnp.zeros_like(pos)
    for e in ends:
        count = count + (pos >= e).astype(jnp.int32)
    return jnp.where(pos < 0, -1, count)


def pack_kernel(k_ref, v_ref, kv_ref):
    kv_ref[:, :HEAD_DIM] = k_ref[...]
    kv_ref[:, HEAD_DIM:] = v_ref[...]


def relay_kernel(a_ref, after, o_ref):
    o_ref[...] = a_ref[...]


def join_kernel(a_ref, b_ref, o_ref):
    rows = a_ref.shape[0]
    o_ref[:rows, :] = a_ref[...]
    o_ref[rows:, :] = b_ref[...]


def edge_kernel(own_ref, last_ref, b_ref, o1, o2, o3):
    xi = place_of()[1]
    rows = own_ref.shape[0]
    for k, out in ((1, o1), (2, o2), (3, o3)):
        out[rows:, :] = b_ref[...]

        @pl.when(xi + k < NX)
        def _():
            out[:rows, :] = own_ref[...]

        @pl.when(xi + k >= NX)
        def _():
            out[:rows, :] = last_ref[...]


def state_kernel(lengths, x_ref, b_ref, raw_ref, bias_ref, alog_ref,
                 o0, o1, o2, o3, d_ref, cumt_ref, lead_ref, scr):
    heads, toks = raw_ref.shape
    lanes = x_ref.shape[1]
    zi, xi = place_of()
    first = (zi * NX + xi) * toks
    ends = ends_of(lengths)
    width = jax.nn.softplus(raw_ref[...].T + bias_ref[...])
    rate2 = width * (-LOG2E * jnp.exp(alog_ref[...]))
    lower = (iota((toks, toks), 0) >= iota((toks, toks), 1)).astype(F32).astype(BF16)
    cumt = sum(jnp.dot(lower, part, preferred_element_type=F32) for part in split3(rate2))
    d_ref[...] = (cumt - jnp.log2(width)).T
    cumt_ref[...] = cumt
    before = rollout_at(first - 1, ends)
    last = rollout_at(first + (toks - 1), ends)
    roll = rollout_at(first + iota((toks, heads), 0), ends)
    lead_ref[...] = jnp.where(roll == before, jnp.exp2(cumt), 0.0)
    end = cumt[toks - 1:toks, :]
    tail = jnp.where(roll == last, jnp.exp2(end - cumt), 0.0) * width
    expand = expander(heads, lanes)
    xw = (spread(tail, expand, 2) * x_ref[...].astype(F32)).astype(BF16)
    state = lax.dot_general(b_ref[...], xw, (((0,), (0,)), ((), ())), preferred_element_type=F32)
    through = jnp.where(last == before, jnp.exp2(end), 0.0)
    th = [jnp.dot(part, expand, preferred_element_type=F32) for part in split3(through)]
    row = iota((EXTRA, lanes), 0)
    extra = jnp.where(row == 0, th[0], jnp.where(row == 1, th[1], jnp.where(row == 2, th[2], 0.0)))
    whole = jnp.concatenate([state, extra], axis=0).astype(BF16)
    for q in range(NX):
        scr[q] = whole[:, q * QUARTER:(q + 1) * QUARTER]
    for k, out in enumerate((o0, o1, o2, o3)):
        out[...] = scr[lax.rem(xi + k, NX)]


def with_decay(ref, state, decay):
    hi, mid, low = split3(decay)
    row = iota((EXTRA, QUARTER), 0)
    extra = jnp.where(row == 0, hi.astype(F32), jnp.where(row == 1, mid.astype(F32), jnp.where(row == 2, low.astype(F32), 0.0)))
    ref[:STATE, :] = state.astype(BF16)
    ref[STATE:, :] = extra.astype(BF16)


def decay_in(tail):
    tail = tail.astype(F32)
    return tail[0:1] + tail[1:2] + tail[2:3]


def row_kernel(a0, a1, a2, a3, after, p_ref, t_ref, pth_ref, scr):
    zi, xi = place_of()
    for k, a in enumerate((a0, a1, a2, a3)):
        scr[lax.rem(xi - k + NX, NX)] = a[...]
    total = jnp.zeros((STATE, QUARTER), F32)
    through = jnp.ones((1, QUARTER), F32)
    for j in range(NX):
        p_ref[j] = total.astype(BF16)
        pth_ref[j] = jnp.broadcast_to(through, (8, QUARTER))
        one = decay_in(scr[j, STATE:STATE + EXTRA, :])
        total = one * total + scr[j, :STATE, :].astype(F32)
        through = through * one
    with_decay(t_ref, total, jnp.where(zi > 0, through, 0.0))


def pair_kernel(t_ref, came_ref, o_ref):
    through = decay_in(t_ref[STATE:, :])
    total = t_ref[:STATE, :].astype(F32) + through * came_ref[:STATE, :].astype(F32)
    with_decay(o_ref, total, through * decay_in(came_ref[STATE:, :]))


def back_kernel(p_ref, pth_ref, near_ref, far_ref, o0, o1, o2, o3):
    zi, xi = place_of()
    came = near_ref[:STATE, :].astype(F32) + decay_in(near_ref[STATE:, :]) * far_ref[:STATE, :].astype(F32)
    came = jnp.where(zi > 0, came, 0.0)
    for k, out in enumerate((o0, o1, o2, o3)):
        j = lax.rem(xi + k, NX)
        out[...] = (p_ref[j].astype(F32) + pth_ref[j][0:1] * came).astype(BF16)


def local_kernel(lengths, x_ref, b_ref, c_ref, d_ref, cumt_ref, skip_ref, y_ref, token_ref):
    token_ref[...] = jnp.zeros_like(token_ref)
    toks, lanes = x_ref.shape
    heads = d_ref.shape[0]
    half = toks // 2
    zi, xi = place_of()
    first = (zi * NX + xi) * toks
    ends = ends_of(lengths)
    roll_t = rollout_at(first + iota((toks, toks), 0), ends)
    roll_s = rollout_at(first + iota((toks, toks), 1), ends)
    seen = (roll_t == roll_s) & (iota((toks, toks), 0) >= iota((toks, toks), 1))
    inner = lax.dot_general(c_ref[...], b_ref[...], (((1,), (1,)), ((), ())), preferred_element_type=F32)
    inner = jnp.where(seen, inner, 0.0)
    left = iota((half, 128), 1) < HEAD_P
    skip = spread(skip_ref[...], expander(heads, lanes))
    d_all = d_ref[...]
    cumt = cumt_ref[...]
    for pair in range(heads // 2):
        cols = slice(pair * 128, (pair + 1) * 128)
        x_pair = x_ref[:, cols]
        for rows, width in ((slice(0, half), half), (slice(half, toks), toks)):
            res = []
            for h in (2 * pair, 2 * pair + 1):
                diff = cumt[rows, h:h + 1] - d_all[h:h + 1, :width]
                mix = (jnp.exp2(jnp.minimum(diff, 64.0)) * inner[rows, :width]).astype(BF16)
                res.append(jnp.dot(mix, x_pair[:width], preferred_element_type=F32))
            y_ref[rows, cols] = jnp.where(left, res[0], res[1]) + skip[:, cols] * x_pair[rows].astype(F32)


def gate_kernel(y_ref, c_ref, lead_ref, gate_ref, gain_ref, i0, i1, i2, i3, out_ref, scr):
    toks, lanes = y_ref.shape
    heads = lead_ref.shape[1]
    xi = place_of()[1]
    for k, a in enumerate((i0, i1, i2, i3)):
        scr[lax.rem(xi - k + NX, NX)] = a[...]
    expand = expander(heads, lanes)
    square = jnp.zeros((toks, 1), F32)
    held = []
    for q in range(NX):
        cols = slice(q * QUARTER, (q + 1) * QUARTER)
        carried = jnp.dot(c_ref[...], scr[q], preferred_element_type=F32)
        lead = spread(lead_ref[...], expand[:, cols], 2)
        v = gate_ref[:, cols].astype(F32)
        gated = (y_ref[:, cols] + lead * carried) * (v / (1.0 + jnp.exp(-v)))
        square = square + jnp.sum(gated * gated, axis=1, keepdims=True)
        held.append(gated)
    factor = lax.rsqrt(square * (1.0 / lanes) + EPS)
    for q in range(NX):
        cols = slice(q * QUARTER, (q + 1) * QUARTER)
        out_ref[:, cols] = (held[q] * factor * gain_ref[:, cols]).astype(BF16)


def fill(lengths, first, slots, k_buf, v_buf):
    toks = k_buf.shape[1]
    lane = iota((toks, HEAD_DIM), 1)
    row = iota((toks, HEAD_DIM), 0)
    ones = (lane == 0).astype(F32).astype(BF16)
    ends = ends_of(lengths)
    begins = (0,) + ends[:3]
    lane_row = iota((1, HEAD_DIM), 1)
    low = jnp.zeros((1, HEAD_DIM), jnp.int32)
    high = low
    for r in range(4):
        low = jnp.where(lane_row == r, begins[r], low)
        high = jnp.where(lane_row == r, ends[r], high)
    for i, (slot, kv) in enumerate(slots):
        start = first + (slot - 16) * toks
        k_buf[i, :, :HEAD_DIM] = kv[:, :HEAD_DIM]
        v_buf[i, :, :HEAD_DIM] = kv[:, HEAD_DIM:]
        k_buf[i, :, HEAD_DIM:] = jnp.where((row >= low - start) & (row < high - start), 0.0, BIG).astype(BF16)
        v_buf[i, :, HEAD_DIM:] = ones


def fill_queries(ends, first, q_ref, q_buf):
    heads, toks = q_buf.shape[:2]
    lane = iota((toks, HEAD_DIM), 1)
    mine = (rollout_at(first + iota((toks, 1), 0), ends) == lane).astype(F32).astype(BF16)
    for h in range(heads):
        q_buf[h, :, :HEAD_DIM] = q_ref[:, h * HEAD_DIM:(h + 1) * HEAD_DIM]
        q_buf[h, :, HEAD_DIM:] = mine


def over_heads(heads, chunks, q_buf, k_buf, v_buf, s_a, s_b, causal_at, start, finish):
    toks = q_buf.shape[1]
    scale = LOG2E / math.sqrt(HEAD_DIM)
    causal = iota((toks, toks), 0) >= iota((toks, toks), 1)

    def scores(h, buf, j, peak):
        s = lax.dot_general(q_buf[h], k_buf[j], (((1,), (1,)), ((), ())), preferred_element_type=F32)
        if j == causal_at:
            s = jnp.where(causal, s, BIG)
        buf[j] = s
        return jnp.maximum(peak, jnp.maximum(s[:, :128], s[:, 128:]))

    def both(h, buf_now, buf_next, peak):
        top = jnp.max(peak, axis=1, keepdims=True)
        acc = start[1](h, top, scale)
        nxt = jnp.minimum(h + 1, heads - 1)
        peak = start[0](nxt)
        for j in range(chunks):
            peak = scores(nxt, buf_next, j, peak)
            p = jnp.exp2((buf_now[j] - top) * scale).astype(BF16)
            acc = acc + jnp.dot(p, v_buf[j], preferred_element_type=F32)
        finish(h, top, acc)
        return peak

    def two(i, peak):
        peak = both(2 * i, s_a, s_b, peak)
        return both(2 * i + 1, s_b, s_a, peak)

    peak = start[0](0)
    for j in range(chunks):
        peak = scores(0, s_a, j, peak)
    lax.fori_loop(0, heads // 2, two, peak)


def attend_first_kernel(lengths, q_ref, own, z1, z2, z3, g1, g2, g3, after, acc_ref, ml_ref,
                        k_buf, v_buf, q_buf, s_a, s_b):
    heads, toks = q_buf.shape[:2]
    zi, xi = place_of()
    first = (zi * NX + xi) * toks
    ends = ends_of(lengths)
    slots = [(16, own), (12, z1), (8, z2), (4, z3)]
    for k, g in ((1, g1), (2, g2), (3, g3)):
        ahead = xi >= k
        slots.append((jnp.where(ahead, 12 - k, 16 - k), g[0:toks, :]))
        slots.append((jnp.where(ahead, 8 - k, 12 - k), g[toks:2 * toks, :]))
    fill(lengths, first, slots, k_buf, v_buf)
    fill_queries(ends, first, q_ref, q_buf)
    lane = iota((toks, HEAD_DIM), 1)

    def finish(h, top, acc):
        acc_ref[h] = acc[:, :HEAD_DIM]
        ml_ref[h] = jnp.where(lane == 0, acc[:, HEAD_DIM:], top)

    start = (lambda h: jnp.full((toks, HEAD_DIM), BIG, F32),
             lambda h, top, scale: jnp.zeros((toks, 2 * HEAD_DIM), F32))
    over_heads(heads, len(slots), q_buf, k_buf, v_buf, s_a, s_b, 0, start, finish)


def attend_second_kernel(lengths, q_ref, z4, g1, g2, g3, acc_ref, ml_ref, after, out_ref,
                         k_buf, v_buf, q_buf, s_a, s_b):
    heads, toks = q_buf.shape[:2]
    zi, xi = place_of()
    first = (zi * NX + xi) * toks
    ends = ends_of(lengths)
    slots = [(0, z4)]
    for k, g in ((1, g1), (2, g2), (3, g3)):
        ahead = xi >= k
        slots.append((jnp.where(ahead, 16 - k, 4 - k), g[0:toks, :]))
        slots.append((jnp.where(ahead, 4 - k, 8 - k), g[toks:2 * toks, :]))
    fill(lengths, first, slots, k_buf, v_buf)
    fill_queries(ends, first, q_ref, q_buf)
    lane = iota((toks, HEAD_DIM), 1)

    def begin(h, top, scale):
        ml = ml_ref[h]
        old = jnp.exp2((ml[:, 1:2] - top) * scale)
        total = jnp.where(lane == 0, ml, 0.0)
        return jnp.concatenate([acc_ref[h], total], axis=1) * old

    def finish(h, top, acc):
        res = acc[:, :HEAD_DIM] / acc[:, HEAD_DIM:HEAD_DIM + 1]
        out_ref[h] = res.astype(BF16)

    start = (lambda h: jnp.where(lane == 0, BIG, ml_ref[h]), begin)
    over_heads(heads, len(slots), q_buf, k_buf, v_buf, s_a, s_b, None, start, finish)


def project_kernel(a_ref, w_ref, after, send_ref, keep_ref, wide, both):
    h = a_ref.shape[0]
    cols = both.shape[2]
    tp = lax.axis_index("tp")
    y, core = tp // 2, lax.rem(tp, 2)
    for i in range(h):
        wide[:, i * HEAD_DIM:(i + 1) * HEAD_DIM] = a_ref[i]
    for k in range(NY):
        at = pl.multiple_of(lax.rem(y + k, NY) * (2 * cols), 2 * cols)
        for c in range(2):
            both[c] = jnp.dot(wide[...], w_ref[:, pl.ds(at + c * cols, cols)], preferred_element_type=F32).astype(BF16)
        send_ref[k] = both[1 - core]
        keep_ref[k] = both[core]


def vmem(n):
    return [pl.BlockSpec(memory_space=pltpu.VMEM)] * n


def smem(n):
    return [pl.BlockSpec(memory_space=pltpu.SMEM)] * n


def cost(us):
    return pl.CostEstimate(flops=int(us * 1.1e9), transcendentals=0, bytes_accessed=int(us * 3.2e6))


def kept(shape, dtype):
    return pltpu.VMEM(shape, dtype)


def sds(shape, dtype):
    return jax.ShapeDtypeStruct(shape, dtype)


def far(a):
    return pltpu.with_memory_space_constraint(a, pltpu.HBM)


def params(mib):
    return pltpu.CompilerParams(vmem_limit_bytes=mib * 1024 * 1024)


def near(a):
    return pltpu.with_memory_space_constraint(a, pltpu.VMEM)


def x_shift(k):
    return [(NX * z + x, NX * z + (x + k) % NX) for z in range(NZ) for x in range(NX)]


def y_shift(k):
    return [(2 * y + c, 2 * ((y + k) % NY) + c) for y in range(NY) for c in range(2)]


def z_shift(k):
    return [(NX * z + x, NX * ((z + k) % NZ) + x) for z in range(NZ) for x in range(NX)]


TWIN = [(i, i ^ 1) for i in range(2 * NY)]


def body(mixer_input, gate_input, input_map, output_map, step_raw, step_bias, decay_log, skip_gain,
         norm_gain, queries, key_heads, value_heads, out_weight, rollout_lengths):
    toks, lanes = mixer_input.shape
    heads = step_raw.shape[0]
    msg = kept((STATE + EXTRA, QUARTER), BF16)
    quarter = kept((STATE, QUARTER), BF16)

    anywhere = [pl.BlockSpec(memory_space=pl.ANY)]
    chunk = kept((toks, 2 * HEAD_DIM), BF16)
    chunks = kept((2 * toks, 2 * HEAD_DIM), BF16)
    one = pl.BlockSpec(memory_space=pltpu.VMEM)
    own = pl.pallas_call(
        pack_kernel, in_specs=vmem(2), out_specs=one, out_shape=chunk,
        compiler_params=params(4), cost_estimate=cost(0.5), name="pack",
    )(far(key_heads), far(value_heads))
    zs = [own, lax.ppermute(own, "ctx", z_shift(1))]
    o0, o1, o2, o3, dd, cumt, lead = pl.pallas_call(
        state_kernel,
        in_specs=smem(1) + vmem(5),
        out_specs=vmem(7),
        out_shape=[msg] * 4 + [kept((heads, toks), F32), kept((toks, heads), F32), kept((toks, heads), F32)],
        scratch_shapes=[pltpu.VMEM((NX, STATE + EXTRA, QUARTER), BF16)],
        compiler_params=params(16),
        cost_estimate=cost(3),
        name="chunk_states",
    )(*map(far, (rollout_lengths, mixer_input, input_map, step_raw, step_bias[None, :], decay_log[None, :])))
    came = [o0] + [lax.ppermute(o, "ctx", x_shift(k)) for k, o in ((1, o1), (2, o2), (3, o3))]

    y_local, token = pl.pallas_call(
        local_kernel,
        in_specs=smem(1) + vmem(6),
        out_specs=vmem(2),
        out_shape=[kept((toks, lanes), F32), kept((8, 128), F32)],
        compiler_params=params(16),
        cost_estimate=cost(2.5),
        name="within_chunk",
    )(rollout_lengths, near(mixer_input), near(input_map), near(output_map), *map(near, (dd, cumt)), skip_gain[None, :])

    sent = pl.pallas_call(
        relay_kernel, in_specs=vmem(1) + anywhere, out_specs=one, out_shape=chunk,
        compiler_params=params(4), cost_estimate=cost(0.5), name="relay",
    )(near(zs[1]), token)
    for _ in range(3):
        sent = lax.ppermute(sent, "ctx", z_shift(1))
        zs.append(sent)
    soon = pl.pallas_call(
        join_kernel, in_specs=vmem(2), out_specs=one, out_shape=chunks,
        compiler_params=params(4), cost_estimate=cost(0.5), name="two_chunks",
    )(near(zs[1]), near(zs[2]))
    gs = [lax.ppermute(soon, "ctx", x_shift(k)) for k in (1, 2, 3)]
    later = pl.pallas_call(
        edge_kernel, in_specs=vmem(3), out_specs=vmem(3), out_shape=[chunks] * 3,
        compiler_params=params(6), cost_estimate=cost(0.5), name="edge_chunks",
    )(near(own), near(zs[4]), near(zs[3]))
    gs = gs + [lax.ppermute(a, "ctx", x_shift(k)) for k, a in zip((1, 2, 3), later)]

    prefix, total, pth = pl.pallas_call(
        row_kernel,
        in_specs=vmem(4) + [pl.BlockSpec(memory_space=pl.ANY)],
        out_specs=vmem(3),
        out_shape=[kept((NX, STATE, QUARTER), BF16), msg, kept((NX, 8, QUARTER), F32)],
        scratch_shapes=[pltpu.VMEM((NX, STATE + EXTRA, QUARTER), BF16)],
        compiler_params=params(12),
        cost_estimate=cost(1),
        name="row_scan",
    )(*map(near, came), token)

    once = lax.ppermute(total, "ctx", z_shift(1))
    pair = pl.pallas_call(
        pair_kernel,
        in_specs=vmem(2),
        out_specs=pl.BlockSpec(memory_space=pltpu.VMEM),
        out_shape=msg,
        compiler_params=params(8),
        cost_estimate=cost(0.5),
        name="two_rows",
    )(near(total), near(once))
    twice = lax.ppermute(pair, "ctx", z_shift(1))
    before = lax.ppermute(twice, "ctx", z_shift(2))
    backs = pl.pallas_call(
        back_kernel,
        in_specs=vmem(4),
        out_specs=vmem(4),
        out_shape=[quarter] * 4,
        compiler_params=params(8),
        cost_estimate=cost(1),
        name="row_states",
    )(*map(near, (prefix, pth, twice, before)))
    incoming = [backs[0]] + [lax.ppermute(backs[k], "ctx", x_shift(k)) for k in (1, 2, 3)]

    q_heads = queries.shape[1] // HEAD_DIM
    def scratch(chunks):
        wide = pltpu.VMEM((chunks, toks, 2 * HEAD_DIM), BF16)
        logits = pltpu.VMEM((chunks, toks, toks), F32)
        return [wide, wide, pltpu.VMEM((q_heads, toks, 2 * HEAD_DIM), BF16), logits, logits]

    acc, ml = pl.pallas_call(
        attend_first_kernel,
        in_specs=smem(1) + vmem(8) + anywhere,
        out_specs=vmem(2),
        out_shape=[kept((q_heads, toks, HEAD_DIM), F32)] * 2,
        scratch_shapes=scratch(10),
        compiler_params=params(24),
        cost_estimate=cost(10),
        name="attend_first",
    )(rollout_lengths, queries, *map(near, (*zs[:4], *gs[:3])), pair)
    attended = pl.pallas_call(
        attend_second_kernel,
        in_specs=smem(1) + vmem(7) + anywhere,
        out_specs=pl.BlockSpec(memory_space=pltpu.VMEM),
        out_shape=kept((q_heads, toks, HEAD_DIM), BF16),
        scratch_shapes=scratch(7),
        compiler_params=params(20),
        cost_estimate=cost(8),
        name="attend_second",
    )(rollout_lengths, queries, *map(near, (zs[4], *gs[3:], acc, ml)), twice)

    cols = out_weight.shape[1] // (2 * NY)
    send, keep = pl.pallas_call(
        project_kernel,
        in_specs=vmem(2) + anywhere,
        out_specs=vmem(2),
        out_shape=[kept((NY, toks, cols), BF16)] * 2,
        scratch_shapes=[pltpu.VMEM((toks, q_heads * HEAD_DIM), BF16), pltpu.VMEM((2, toks, cols), BF16)],
        compiler_params=params(16),
        cost_estimate=cost(3),
        name="project",
    )(near(attended), near(out_weight), before)
    twin = lax.ppermute(send, "tp", TWIN)
    summed = [keep[k].astype(F32) + twin[k].astype(F32) for k in range(NY)]
    block_out = summed[0]
    for k in (1, 2, 3):
        block_out = block_out + lax.ppermute(summed[k].astype(BF16), "tp", y_shift(k)).astype(F32)
    block_out = block_out.astype(BF16)

    mamba_out = pl.pallas_call(
        gate_kernel,
        in_specs=vmem(9),
        out_specs=pl.BlockSpec(memory_space=pltpu.VMEM),
        out_shape=sds((toks, lanes), BF16),
        scratch_shapes=[pltpu.VMEM((NX, STATE, QUARTER), BF16)],
        compiler_params=params(16),
        cost_estimate=cost(2.5),
        name="carry_gate_norm",
    )(*map(near, (y_local, output_map, lead, gate_input)), norm_gain[None, :], *map(near, incoming))
    return (mamba_out, block_out)


def solution(mesh):
    both = P("ctx", "tp")
    return jax.shard_map(
        body,
        mesh=mesh,
        in_specs=(both, both, both, both, P("tp", "ctx"), P("tp"), P("tp"), P("tp"), P("tp"),
                  both, both, both, P("tp", None), P()),
        out_specs=(both, both),
        check_vma=False,
    )
```

time: 154 us -> 93.8 us (0.61)
  the two profiles are of different devices: /device:TPU:64 before, /device:TPU:1 now
where the time goes in v2:
time: 93.8 us; the launch traced here: 93.7 us
  starting transfers between devices  34.7 us (37%)
  Pallas kernels  28.5 us (30%)
  waiting for transfers between devices  28.4 us (30%)
  other arithmetic  1.09 us (1%)
    ppermute x3, waiting for transfers between devices, body(): sent = lax.ppermute(sent, 'ctx', z_shift(1))  13.2 us
    pallas_call x1, Pallas kernels, body(): pl.pallas_call(attend_first_kernel, in_specs=smem(1) + vmem(8) + anywhere...  8.65 us
    ppermute x1, starting transfers between devices, body(): twin = lax.ppermute(send, 'tp', TWIN)  8.57 us
    ppermute x3, waiting for transfers between devices, body(): lax.ppermute(backs[k], 'ctx', x_shift(k))  7.41 us
    pallas_call x1, Pallas kernels, body(): pl.pallas_call(attend_second_kernel, in_specs=smem(1) + vmem(7) + anywher...  7.1 us
    ppermute x3, starting transfers between devices, body(): lax.ppermute(o, 'ctx', x_shift(k))  5.73 us
    ppermute x3, starting transfers between devices, body(): lax.ppermute(a, 'ctx', x_shift(k))  5.25 us
    ppermute x3, starting transfers between devices, body(): lax.ppermute(summed[k].astype(BF16), 'tp', y_shift(k)).astype(F32)  4.44 us
  transfers between devices with their start and end apart: 23, of which 7 were waited for; matrix products, arithmetic and copies ran while one was open for 0% of the time, Pallas kernels for 24%

profile of v2, /device:TPU:1, one launch (start us, length us, event | category | flops | bytes accessed | tf_op | source)
XLA Modules:
  0.0 93.7 jit_solution(17236026616940328089)
XLA Ops:
  0.7 2.9 %chunk_states.1 = (bf16[272,512]{1,0:T(8,128)(2,1)S(1)}, bf16[272,512]{1,0:T(8,128)(2,1)S(1)}, bf16[272,512]{1,0:T(8,128)(2,1)S(1)}, bf16[272,512]{1,0:T(8,128)(...) custom-call(s32[4]{0:T(128)} %lengths.7, bf16[256,2048]{1,0:T(8,128)(2,1)} %x_ref.3, ...), custom_call_target="tpu_custom_call" | custom-call | flops 3300000000 | bytes 9600000 | tf_op jit(solution)/shard_map/chunk_states/pallas_call | solution.py:421
  3.6 2.1 %collective-permute-start = (bf16[272,512]{1,0:T(8,128)(2,1)S(1)}, bf16[272,512]{1,0:T(8,128)(2,1)S(1)}, u32[]{:S(2)}, u32[]{:S(2)}) collective-permute-start(bf16[272,512]{1,0:T(8,128)(2,1)S(1)} %get-tuple-element.30), channel_id=1, source_target_pairs={{0,8},{8,16},{16,24},{24,0},{32,40},{40,48},{48,56},{56,32},{64,72... | collective-permute-start | bytes 835592 | tf_op jit(solution)/shard_map/ppermute | solution.py:431
  5.7 2.5 %collective-permute-start.1 = (bf16[272,512]{1,0:T(8,128)(2,1)S(1)}, bf16[272,512]{1,0:T(8,128)(2,1)S(1)}, u32[]{:S(2)}, u32[]{:S(2)}) collective-permute-start(bf16[272,512]{1,0:T(8,128)(2,1)S(1)} %get-tuple-element.31), channel_id=1, source_target_pairs={{0,16},{8,24},{16,0},{24,8},{32,48},{40,56},{48,32},{56,40},{64,80... | collective-permute-start | bytes 835592 | tf_op jit(solution)/shard_map/ppermute | solution.py:431
  8.2 1.2 %collective-permute-start.2 = (bf16[272,512]{1,0:T(8,128)(2,1)S(1)}, bf16[272,512]{1,0:T(8,128)(2,1)S(1)}, u32[]{:S(2)}, u32[]{:S(2)}) collective-permute-start(bf16[272,512]{1,0:T(8,128)(2,1)S(1)} %get-tuple-element.32), channel_id=1, source_target_pairs={{0,24},{8,0},{16,8},{24,16},{32,56},{40,32},{48,40},{56,48},{64,88... | collective-permute-start | bytes 835592 | tf_op jit(solution)/shard_map/ppermute | solution.py:431
  9.4 0.9 pack.1.own_ref.own
  10.3 1.7 %collective-permute-start.9 = (bf16[256,256]{1,0:T(8,128)(2,1)S(1)}, bf16[256,256]{1,0:T(8,128)(2,1)S(1)}, u32[]{:S(2)}, u32[]{:S(2)}) collective-permute-start(bf16[256,256]{1,0:T(8,128)(2,1)S(1)} %pack.1.own_ref.own), channel_id=1, source_target_pairs={{0,32},{8,40},{16,48},{24,56},{32,64},{40,72},{48,80},{56,88},{64,... | collective-permute-start | bytes 393224 | tf_op jit(solution)/shard_map/ppermute | solution.py:420
  12.0 0.0 copy-done.4
  12.0 2.5 %within_chunk.1 = (f32[256,2048]{1,0:T(8,128)S(1)}, f32[8,128]{1,0:T(8,128)S(1)}) custom-call(s32[4]{0:T(128)S(1)} %copy-done.7, bf16[256,2048]{1,0:T(8,128)(2,1)S(1)} %copy-done, bf16[256,256]{1,0:T(8,128)(2,1)S(1)} %copy-done.3, bf16[256,256]{1,0:T(8,128)(2,1)S(1)} %copy-done.4, f32[32,256]{1,0:T(8,128)S(1)} %get-tuple-element.25.d_ref, ...), custom_call_target="tpu_custom_call" | custom-call | flops 2750000128 | bytes 8000000 | tf_op jit(solution)/shard_map/within_chunk/pallas_call | solution.py:433
  14.5 0.0 copy-start.2
  14.5 4.0 %collective-permute-done.9.a_ref.z1 = bf16[256,256]{1,0:T(8,128)(2,1)S(1)} collective-permute-done((bf16[256,256]{1,0:T(8,128)(2,1)S(1)}, bf16[256,256]{1,0:T(8,128)(2,1)S(1)}, u32[]{:S(2)}, u32[]{:S(2)}) %collective-permute-start.9) | collective-permute-done | bytes 131104 | tf_op jit(solution)/shard_map/ppermute | solution.py:420
  18.6 0.1 collective-permute-start.10
  18.7 5.0 %collective-permute-done.10.b_ref.z2 = bf16[256,256]{1,0:T(8,128)(2,1)S(1)} collective-permute-done((bf16[256,256]{1,0:T(8,128)(2,1)S(1)}, bf16[256,256]{1,0:T(8,128)(2,1)S(1)}, u32[]{:S(2)}, u32[]{:S(2)}) %collective-permute-start.10) | collective-permute-done | bytes 131104 | tf_op jit(solution)/shard_map/ppermute | solution.py:448
  23.7 0.0 collective-permute-start.11
  23.7 0.0 collective-permute-done.a1
  23.7 0.0 collective-permute-done.1.a2
  23.7 0.0 collective-permute-done.2.a3
  23.7 0.6 row_scan.1
  24.3 0.1 collective-permute-start.3
  24.4 0.1 collective-permute-start.16
  24.5 2.3 %collective-permute-start.17 = (bf16[512,256]{1,0:T(8,128)(2,1)S(1)}, bf16[512,256]{1,0:T(8,128)(2,1)S(1)}, u32[]{:S(2)}, u32[]{:S(2)}) collective-permute-start(bf16[512,256]{1,0:T(8,128)(2,1)S(1)} %two_chunks.1), channel_id=1, source_target_pairs={{0,16},{8,24},{16,0},{24,8},{32,48},{40,56},{48,32},{56,40},{64,80... | collective-permute-start | bytes 786440 | tf_op jit(solution)/shard_map/ppermute | solution.py:454
  26.8 0.3 collective-permute-start.18
  27.1 1.6 %collective-permute-done.11.b_ref.z3 = bf16[256,256]{1,0:T(8,128)(2,1)S(1)} collective-permute-done((bf16[256,256]{1,0:T(8,128)(2,1)S(1)}, bf16[256,256]{1,0:T(8,128)(2,1)S(1)}, u32[]{:S(2)}, u32[]{:S(2)}) %collective-permute-start.11) | collective-permute-done | bytes 131104 | tf_op jit(solution)/shard_map/ppermute | solution.py:448
  28.7 0.2 collective-permute-start.12
  28.9 6.6 %collective-permute-done.12.last_ref.z4 = bf16[256,256]{1,0:T(8,128)(2,1)S(1)} collective-permute-done((bf16[256,256]{1,0:T(8,128)(2,1)S(1)}, bf16[256,256]{1,0:T(8,128)(2,1)S(1)}, u32[]{:S(2)}, u32[]{:S(2)}) %collective-permute-start.12) | collective-permute-done | bytes 131104 | tf_op jit(solution)/shard_map/ppermute | solution.py:448
  35.5 0.1 edge_chunks.1
  35.5 1.1 %collective-permute-start.13 = (bf16[512,256]{1,0:T(8,128)(2,1)S(1)}, bf16[512,256]{1,0:T(8,128)(2,1)S(1)}, u32[]{:S(2)}, u32[]{:S(2)}) collective-permute-start(bf16[512,256]{1,0:T(8,128)(2,1)S(1)} %get-tuple-element.41), channel_id=1, source_target_pairs={{0,8},{8,16},{16,24},{24,0},{32,40},{40,48},{48,56},{56,32},{64,72... | collective-permute-start | bytes 786440 | tf_op jit(solution)/shard_map/ppermute | solution.py:459
  36.7 0.0 collective-permute-done.3.came_ref
  36.7 4.0 %collective-permute-start.14 = (bf16[512,256]{1,0:T(8,128)(2,1)S(1)}, bf16[512,256]{1,0:T(8,128)(2,1)S(1)}, u32[]{:S(2)}, u32[]{:S(2)}) collective-permute-start(bf16[512,256]{1,0:T(8,128)(2,1)S(1)} %get-tuple-element.42), channel_id=1, source_target_pairs={{0,16},{8,24},{16,0},{24,8},{32,48},{40,56},{48,32},{56,40},{64,80... | collective-permute-start | bytes 786440 | tf_op jit(solution)/shard_map/ppermute | solution.py:459
  40.7 0.1 two_rows.1.after
  40.8 0.0 collective-permute-done.16.g1
  40.8 0.0 slice-start.1
  40.8 0.1 collective-permute-start.15
  40.9 0.0 collective-permute-done.17.g2
  40.9 0.1 collective-permute-start.4
  41.0 0.0 collective-permute-done.18.g3
  41.1 8.6 %attend_first.1 = (f32[8,256,128]{2,1,0:T(8,128)S(1)}, f32[8,256,128]{2,1,0:T(8,128)S(1)}) custom-call(s32[4]{0:T(128)S(1)} %copy-done.7, bf16[256,1024]{1,0:T(8,128)(2,1)S(1)} %copy-done.2, bf16[256,256]{1,0:T(8,128)(2,1)S(1)} %pack.1.own_ref.own, bf16[256,256]{1,0:T(8,128)(2,1)S(1)} %collective-permute-done.9.a_ref.z1, ...), custom_call_target="tpu_custom_call" | custom-call | flops 11000000512 | bytes 32000000 | tf_op jit(solution)/shard_map/attend_first/pallas_call | solution.py:501
  49.7 0.0 collective-permute-done.4.near_ref.after
  49.7 2.6 %collective-permute-start.5 = (bf16[272,512]{1,0:T(8,128)(2,1)S(1)}, bf16[272,512]{1,0:T(8,128)(2,1)S(1)}, u32[]{:S(2)}, u32[]{:S(2)}) collective-permute-start(bf16[272,512]{1,0:T(8,128)(2,1)S(1)} %collective-permute-done.4.near_ref.after), channel_id=1, source_target_pairs={{0,64},{8,72},{16,80},{24,88},{32,96},{40,104},{48,112},{56,120},{... | collective-permute-start | bytes 835592 | tf_op jit(solution)/shard_map/ppermute | solution.py:483
  52.3 0.0 collective-permute-done.13.g1
  52.3 0.0 collective-permute-done.14.g2
  52.3 0.0 collective-permute-done.15.g3
  52.3 7.1 %attend_second.1.a_ref = bf16[8,256,128]{2,1,0:T(8,128)(2,1)S(1)} custom-call(s32[4]{0:T(128)S(1)} %copy-done.7, bf16[256,1024]{1,0:T(8,128)(2,1)S(1)} %copy-done.2, bf16[256,256]{1,0:T(8,128)(2,1)S(1)} %collective-permute-done.12.last_ref.z4, bf16[512,256]{1,0:T(8,128)(2,1)S(1)} %collective-permute-done.13.g1, ...), custom_call_target="tpu_custom_call" | custom-call | flops 8800000000 | bytes 25600000 | tf_op jit(solution)/shard_map/attend_second/pallas_call | solution.py:511
  59.4 0.0 copy-start.1
  59.4 0.0 copy-start.5
  59.4 0.0 collective-permute-done.5.far_ref.after
  59.5 2.8 %project.1 = (bf16[4,256,512]{2,1,0:T(8,128)(2,1)S(1)}, bf16[4,256,512]{2,1,0:T(8,128)(2,1)S(1)}) custom-call(bf16[8,256,128]{2,1,0:T(8,128)(2,1)S(1)} %attend_second.1.a_ref, bf16[1024,4096]{1,0:T(8,128)(2,1)S(1)} %bitcast.19, bf16[272,512]{1,0:T(8,128)(2,1)S(1)} %collective-permute-done.5.far_ref.after), custom_call_target="tpu_custom_call" | custom-call | flops 3300000000 | bytes 9600000 | tf_op jit(solution)/shard_map/project/pallas_call | solution.py:523
  62.3 8.6 %collective-permute-start.19 = (bf16[4,256,512]{2,1,0:T(8,128)(2,1)S(1)}, bf16[4,256,512]{2,1,0:T(8,128)(2,1)S(1)}, u32[]{:S(2)}, u32[]{:S(2)}) collective-permute-start(bf16[4,256,512]{2,1,0:T(8,128)(2,1)S(1)} %get-tuple-element.47), channel_id=1, source_target_pairs={{0,1},{1,0},{2,3},{3,2},{4,5},{5,4},{6,7},{7,6},{8,9},{9,8},{10,11... | collective-permute-start | bytes 3145736 | tf_op jit(solution)/shard_map/ppermute | solution.py:533
  70.8 0.3 row_states.1
  71.2 0.5 collective-permute-start.6
  71.7 2.8 %collective-permute-start.7 = (bf16[256,512]{1,0:T(8,128)(2,1)S(1)}, bf16[256,512]{1,0:T(8,128)(2,1)S(1)}, u32[]{:S(2)}, u32[]{:S(2)}) collective-permute-start(bf16[256,512]{1,0:T(8,128)(2,1)S(1)} %get-tuple-element.39), channel_id=1, source_target_pairs={{0,16},{8,24},{16,0},{24,8},{32,48},{40,56},{48,32},{56,40},{64,80... | collective-permute-start | bytes 786440 | tf_op jit(solution)/shard_map/ppermute | solution.py:493
  74.4 0.0 collective-permute-start.8
  74.4 0.0 collective-permute-done.19
  74.4 0.2 fusion.3
  74.7 2.8 %collective-permute-start.22 = (bf16[256,512]{1,0:T(8,128)(2,1)S(1)}, bf16[256,512]{1,0:T(8,128)(2,1)S(1)}, u32[]{:S(2)}, u32[]{:S(2)}) collective-permute-start(bf16[256,512]{1,0:T(8,128)(2,1)S(1)} %get-tuple-element.49), channel_id=1, source_target_pairs={{0,6},{1,7},{2,0},{3,1},{4,2},{5,3},{6,4},{7,5},{8,14},{9,15},{10,... | collective-permute-start | bytes 786440 | tf_op jit(solution)/shard_map/ppermute | solution.py:537
  77.4 0.4 collective-permute-start.21
  77.8 2.6 %collective-permute-done.6.i1 = bf16[256,512]{1,0:T(8,128)(2,1)S(1)} collective-permute-done((bf16[256,512]{1,0:T(8,128)(2,1)S(1)}, bf16[256,512]{1,0:T(8,128)(2,1)S(1)}, u32[]{:S(2)}, u32[]{:S(2)}) %collective-permute-start.6) | collective-permute-done | bytes 262176 | tf_op jit(solution)/shard_map/ppermute | solution.py:493
  80.4 1.3 %collective-permute-start.20 = (bf16[256,512]{1,0:T(8,128)(2,1)S(1)}, bf16[256,512]{1,0:T(8,128)(2,1)S(1)}, u32[]{:S(2)}, u32[]{:S(2)}) collective-permute-start(bf16[256,512]{1,0:T(8,128)(2,1)S(1)} %get-tuple-element.48), channel_id=1, source_target_pairs={{0,2},{1,3},{2,4},{3,5},{4,6},{5,7},{6,0},{7,1},{8,10},{9,11},{10,... | collective-permute-start | bytes 786440 | tf_op jit(solution)/shard_map/ppermute | solution.py:537
  81.7 4.8 %collective-permute-done.7.i2 = bf16[256,512]{1,0:T(8,128)(2,1)S(1)} collective-permute-done((bf16[256,512]{1,0:T(8,128)(2,1)S(1)}, bf16[256,512]{1,0:T(8,128)(2,1)S(1)}, u32[]{:S(2)}, u32[]{:S(2)}) %collective-permute-start.7) | collective-permute-done | bytes 262176 | tf_op jit(solution)/shard_map/ppermute | solution.py:493
  86.5 0.0 collective-permute-done.8.i3
  86.5 2.5 %carry_gate_norm.1 = bf16[256,2048]{1,0:T(8,128)(2,1)} custom-call(f32[256,2048]{1,0:T(8,128)S(1)} %get-tuple-element.27.y_ref, bf16[256,256]{1,0:T(8,128)(2,1)S(1)} %copy-done.4, f32[256,32]{1,0:T(8,128)S(1)} %get-tuple-element.28.lead_ref, bf16[256,2048]{1,0:T(8,128)(2,1)S(1)} %copy-done.1, f32[1,2048]{1,0:T(1,128)S(1)} %bitcast.20, ...), custom_call_target="tpu_custom_call" | custom-call | flops 2750000128 | bytes 8000000 | tf_op jit(solution)/shard_map/carry_gate_norm/pallas_call | solution.py:540
  89.0 0.0 collective-permute-done.22
  89.0 0.0 collective-permute-done.21
  89.0 3.8 %collective-permute-done.20 = bf16[256,512]{1,0:T(8,128)(2,1)S(1)} collective-permute-done((bf16[256,512]{1,0:T(8,128)(2,1)S(1)}, bf16[256,512]{1,0:T(8,128)(2,1)S(1)}, u32[]{:S(2)}, u32[]{:S(2)}) %collective-permute-start.20) | collective-permute-done | bytes 262176 | tf_op jit(solution)/shard_map/ppermute | solution.py:537
  92.8 0.9 fusion.2
  (18 shorter events, 0.1 us)
Async XLA Ops:
  0.6 11.3 %copy-start.7 = (s32[4]{0:T(128)S(1)}, s32[4]{0:T(128)}, u32[]{:S(2)}) copy-start(s32[4]{0:T(128)} %lengths.7) | copy-start | bytes 52
  0.6 11.3 %copy-start = (bf16[256,2048]{1,0:T(8,128)(2,1)S(1)}, bf16[256,2048]{1,0:T(8,128)(2,1)}, u32[]{:S(2)}) copy-start(bf16[256,2048]{1,0:T(8,128)(2,1)} %x_ref.3) | copy-start | bytes 3145732
  0.7 11.3 %copy-start.3 = (bf16[256,256]{1,0:T(8,128)(2,1)S(1)}, bf16[256,256]{1,0:T(8,128)(2,1)}, u32[]{:S(2)}) copy-start(bf16[256,256]{1,0:T(8,128)(2,1)} %b_ref.3) | copy-start | bytes 393220
  0.7 11.3 %copy-start.4 = (bf16[256,256]{1,0:T(8,128)(2,1)S(1)}, bf16[256,256]{1,0:T(8,128)(2,1)}, u32[]{:S(2)}) copy-start(bf16[256,256]{1,0:T(8,128)(2,1)} %c_ref.3) | copy-start | bytes 393220
  0.7 11.3 %copy-start.6 = (f32[32]{0:T(128)S(1)}, f32[32]{0:T(128)}, u32[]{:S(2)}) copy-start(f32[32]{0:T(128)} %param.21) | copy-start | bytes 388
  3.6 20.1 %collective-permute-start = (bf16[272,512]{1,0:T(8,128)(2,1)S(1)}, bf16[272,512]{1,0:T(8,128)(2,1)S(1)}, u32[]{:S(2)}, u32[]{:S(2)}) collective-permute-start(bf16[272,512]{1,0:T(8,128)(2,1)S(1)} %get-tuple-element.30), channel_id=1, source_target_pairs={{0,8},{8,16},{16,24},{24,0},{32,40},{40,48},{48,56},{56,32},{64,72... | collective-permute-start | bytes 835592 | tf_op jit(solution)/shard_map/ppermute | solution.py:431
  5.7 17.9 %collective-permute-start.1 = (bf16[272,512]{1,0:T(8,128)(2,1)S(1)}, bf16[272,512]{1,0:T(8,128)(2,1)S(1)}, u32[]{:S(2)}, u32[]{:S(2)}) collective-permute-start(bf16[272,512]{1,0:T(8,128)(2,1)S(1)} %get-tuple-element.31), channel_id=1, source_target_pairs={{0,16},{8,24},{16,0},{24,8},{32,48},{40,56},{48,32},{56,40},{64,80... | collective-permute-start | bytes 835592 | tf_op jit(solution)/shard_map/ppermute | solution.py:431
  8.2 15.5 %collective-permute-start.2 = (bf16[272,512]{1,0:T(8,128)(2,1)S(1)}, bf16[272,512]{1,0:T(8,128)(2,1)S(1)}, u32[]{:S(2)}, u32[]{:S(2)}) collective-permute-start(bf16[272,512]{1,0:T(8,128)(2,1)S(1)} %get-tuple-element.32), channel_id=1, source_target_pairs={{0,24},{8,0},{16,8},{24,16},{32,56},{40,32},{48,40},{56,48},{64,88... | collective-permute-start | bytes 835592 | tf_op jit(solution)/shard_map/ppermute | solution.py:431
  10.3 8.3 %collective-permute-start.9 = (bf16[256,256]{1,0:T(8,128)(2,1)S(1)}, bf16[256,256]{1,0:T(8,128)(2,1)S(1)}, u32[]{:S(2)}, u32[]{:S(2)}) collective-permute-start(bf16[256,256]{1,0:T(8,128)(2,1)S(1)} %pack.1.own_ref.own), channel_id=1, source_target_pairs={{0,32},{8,40},{16,48},{24,56},{32,64},{40,72},{48,80},{56,88},{64,... | collective-permute-start | bytes 393224 | tf_op jit(solution)/shard_map/ppermute | solution.py:420
  14.5 26.5 %copy-start.2 = (bf16[256,1024]{1,0:T(8,128)(2,1)S(1)}, bf16[256,1024]{1,0:T(8,128)(2,1)}, u32[]{:S(2)}) copy-start(bf16[256,1024]{1,0:T(8,128)(2,1)} %q_ref.3) | copy-start | bytes 1572868
  18.6 5.1 %collective-permute-start.10 = (bf16[256,256]{1,0:T(8,128)(2,1)S(1)}, bf16[256,256]{1,0:T(8,128)(2,1)S(1)}, u32[]{:S(2)}, u32[]{:S(2)}) collective-permute-start(bf16[256,256]{1,0:T(8,128)(2,1)S(1)} %relay.1), channel_id=1, source_target_pairs={{0,32},{8,40},{16,48},{24,56},{32,64},{40,72},{48,80},{56,88},{64,... | collective-permute-start | bytes 393224 | tf_op jit(solution)/shard_map/ppermute | solution.py:448
  23.7 5.0 %collective-permute-start.11 = (bf16[256,256]{1,0:T(8,128)(2,1)S(1)}, bf16[256,256]{1,0:T(8,128)(2,1)S(1)}, u32[]{:S(2)}, u32[]{:S(2)}) collective-permute-start(bf16[256,256]{1,0:T(8,128)(2,1)S(1)} %collective-permute-done.10.b_ref.z2), channel_id=1, source_target_pairs={{0,32},{8,40},{16,48},{24,56},{32,64},{40,72},{48,80},{56,88},{64,... | collective-permute-start | bytes 393224 | tf_op jit(solution)/shard_map/ppermute | solution.py:448
  24.3 12.4 %collective-permute-start.3 = (bf16[272,512]{1,0:T(8,128)(2,1)S(1)}, bf16[272,512]{1,0:T(8,128)(2,1)S(1)}, u32[]{:S(2)}, u32[]{:S(2)}) collective-permute-start(bf16[272,512]{1,0:T(8,128)(2,1)S(1)} %get-tuple-element.36.t_ref), channel_id=1, source_target_pairs={{0,32},{8,40},{16,48},{24,56},{32,64},{40,72},{48,80},{56,88},{64,... | collective-permute-start | bytes 835592 | tf_op jit(solution)/shard_map/ppermute | solution.py:472
  24.4 16.4 %collective-permute-start.16 = (bf16[512,256]{1,0:T(8,128)(2,1)S(1)}, bf16[512,256]{1,0:T(8,128)(2,1)S(1)}, u32[]{:S(2)}, u32[]{:S(2)}) collective-permute-start(bf16[512,256]{1,0:T(8,128)(2,1)S(1)} %two_chunks.1), channel_id=1, source_target_pairs={{0,8},{8,16},{16,24},{24,0},{32,40},{40,48},{48,56},{56,32},{64,72... | collective-permute-start | bytes 786440 | tf_op jit(solution)/shard_map/ppermute | solution.py:454
  24.5 16.4 %collective-permute-start.17 = (bf16[512,256]{1,0:T(8,128)(2,1)S(1)}, bf16[512,256]{1,0:T(8,128)(2,1)S(1)}, u32[]{:S(2)}, u32[]{:S(2)}) collective-permute-start(bf16[512,256]{1,0:T(8,128)(2,1)S(1)} %two_chunks.1), channel_id=1, source_target_pairs={{0,16},{8,24},{16,0},{24,8},{32,48},{40,56},{48,32},{56,40},{64,80... | collective-permute-start | bytes 786440 | tf_op jit(solution)/shard_map/ppermute | solution.py:454
  26.8 14.2 %collective-permute-start.18 = (bf16[512,256]{1,0:T(8,128)(2,1)S(1)}, bf16[512,256]{1,0:T(8,128)(2,1)S(1)}, u32[]{:S(2)}, u32[]{:S(2)}) collective-permute-start(bf16[512,256]{1,0:T(8,128)(2,1)S(1)} %two_chunks.1), channel_id=1, source_target_pairs={{0,24},{8,0},{16,8},{24,16},{32,56},{40,32},{48,40},{56,48},{64,88... | collective-permute-start | bytes 786440 | tf_op jit(solution)/shard_map/ppermute | solution.py:454
  28.7 6.8 %collective-permute-start.12 = (bf16[256,256]{1,0:T(8,128)(2,1)S(1)}, bf16[256,256]{1,0:T(8,128)(2,1)S(1)}, u32[]{:S(2)}, u32[]{:S(2)}) collective-permute-start(bf16[256,256]{1,0:T(8,128)(2,1)S(1)} %collective-permute-done.11.b_ref.z3), channel_id=1, source_target_pairs={{0,32},{8,40},{16,48},{24,56},{32,64},{40,72},{48,80},{56,88},{64,... | collective-permute-start | bytes 393224 | tf_op jit(solution)/shard_map/ppermute | solution.py:448
  35.5 16.8 %collective-permute-start.13 = (bf16[512,256]{1,0:T(8,128)(2,1)S(1)}, bf16[512,256]{1,0:T(8,128)(2,1)S(1)}, u32[]{:S(2)}, u32[]{:S(2)}) collective-permute-start(bf16[512,256]{1,0:T(8,128)(2,1)S(1)} %get-tuple-element.41), channel_id=1, source_target_pairs={{0,8},{8,16},{16,24},{24,0},{32,40},{40,48},{48,56},{56,32},{64,72... | collective-permute-start | bytes 786440 | tf_op jit(solution)/shard_map/ppermute | solution.py:459
  36.7 15.6 %collective-permute-start.14 = (bf16[512,256]{1,0:T(8,128)(2,1)S(1)}, bf16[512,256]{1,0:T(8,128)(2,1)S(1)}, u32[]{:S(2)}, u32[]{:S(2)}) collective-permute-start(bf16[512,256]{1,0:T(8,128)(2,1)S(1)} %get-tuple-element.42), channel_id=1, source_target_pairs={{0,16},{8,24},{16,0},{24,8},{32,48},{40,56},{48,32},{56,40},{64,80... | collective-permute-start | bytes 786440 | tf_op jit(solution)/shard_map/ppermute | solution.py:459
  40.7 18.7 %slice-start = ((s8[8388608]{0:T(1024)(128)(4,1)}), s8[4194304]{0:T(1024)(128)(4,1)S(1)}, s32[]{:S(2)}) async-start(s8[8388608]{0:T(1024)(128)(4,1)} %bitcast.18), calls=%async_computation | async-start | bytes 8388608
  40.8 18.6 %slice-start.1 = ((s8[8388608]{0:T(1024)(128)(4,1)}), s8[4194304]{0:T(1024)(128)(4,1)S(1)}, s32[]{:S(2)}) async-start(s8[8388608]{0:T(1024)(128)(4,1)} %bitcast.18), calls=%async_computation.1 | async-start | bytes 8388608
  40.8 11.5 %collective-permute-start.15 = (bf16[512,256]{1,0:T(8,128)(2,1)S(1)}, bf16[512,256]{1,0:T(8,128)(2,1)S(1)}, u32[]{:S(2)}, u32[]{:S(2)}) collective-permute-start(bf16[512,256]{1,0:T(8,128)(2,1)S(1)} %get-tuple-element.43), channel_id=1, source_target_pairs={{0,24},{8,0},{16,8},{24,16},{32,56},{40,32},{48,40},{56,48},{64,88... | collective-permute-start | bytes 786440 | tf_op jit(solution)/shard_map/ppermute | solution.py:459
  40.9 8.8 %collective-permute-start.4 = (bf16[272,512]{1,0:T(8,128)(2,1)S(1)}, bf16[272,512]{1,0:T(8,128)(2,1)S(1)}, u32[]{:S(2)}, u32[]{:S(2)}) collective-permute-start(bf16[272,512]{1,0:T(8,128)(2,1)S(1)} %two_rows.1.after), channel_id=1, source_target_pairs={{0,32},{8,40},{16,48},{24,56},{32,64},{40,72},{48,80},{56,88},{64,... | collective-permute-start | bytes 835592 | tf_op jit(solution)/shard_map/ppermute | solution.py:482
  49.7 9.7 %collective-permute-start.5 = (bf16[272,512]{1,0:T(8,128)(2,1)S(1)}, bf16[272,512]{1,0:T(8,128)(2,1)S(1)}, u32[]{:S(2)}, u32[]{:S(2)}) collective-permute-start(bf16[272,512]{1,0:T(8,128)(2,1)S(1)} %collective-permute-done.4.near_ref.after), channel_id=1, source_target_pairs={{0,64},{8,72},{16,80},{24,88},{32,96},{40,104},{48,112},{56,120},{... | collective-permute-start | bytes 835592 | tf_op jit(solution)/shard_map/ppermute | solution.py:483
  59.4 27.1 %copy-start.1 = (bf16[256,2048]{1,0:T(8,128)(2,1)S(1)}, bf16[256,2048]{1,0:T(8,128)(2,1)}, u32[]{:S(2)}) copy-start(bf16[256,2048]{1,0:T(8,128)(2,1)} %gate_ref.1) | copy-start | bytes 3145732
  59.4 27.1 %copy-start.5 = (f32[2048]{0:T(1024)S(1)}, f32[2048]{0:T(1024)}, u32[]{:S(2)}) copy-start(f32[2048]{0:T(1024)} %param.22) | copy-start | bytes 24580
  62.3 12.2 %collective-permute-start.19 = (bf16[4,256,512]{2,1,0:T(8,128)(2,1)S(1)}, bf16[4,256,512]{2,1,0:T(8,128)(2,1)S(1)}, u32[]{:S(2)}, u32[]{:S(2)}) collective-permute-start(bf16[4,256,512]{2,1,0:T(8,128)(2,1)S(1)} %get-tuple-element.47), channel_id=1, source_target_pairs={{0,1},{1,0},{2,3},{3,2},{4,5},{5,4},{6,7},{7,6},{8,9},{9,8},{10,11... | collective-permute-start | bytes 3145736 | tf_op jit(solution)/shard_map/ppermute | solution.py:533
  71.2 9.2 %collective-permute-start.6 = (bf16[256,512]{1,0:T(8,128)(2,1)S(1)}, bf16[256,512]{1,0:T(8,128)(2,1)S(1)}, u32[]{:S(2)}, u32[]{:S(2)}) collective-permute-start(bf16[256,512]{1,0:T(8,128)(2,1)S(1)} %get-tuple-element.38), channel_id=1, source_target_pairs={{0,8},{8,16},{16,24},{24,0},{32,40},{40,48},{48,56},{56,32},{64,72... | collective-permute-start | bytes 786440 | tf_op jit(solution)/shard_map/ppermute | solution.py:493
  71.7 14.8 %collective-permute-start.7 = (bf16[256,512]{1,0:T(8,128)(2,1)S(1)}, bf16[256,512]{1,0:T(8,128)(2,1)S(1)}, u32[]{:S(2)}, u32[]{:S(2)}) collective-permute-start(bf16[256,512]{1,0:T(8,128)(2,1)S(1)} %get-tuple-element.39), channel_id=1, source_target_pairs={{0,16},{8,24},{16,0},{24,8},{32,48},{40,56},{48,32},{56,40},{64,80... | collective-permute-start | bytes 786440 | tf_op jit(solution)/shard_map/ppermute | solution.py:493
  74.4 12.1 %collective-permute-start.8 = (bf16[256,512]{1,0:T(8,128)(2,1)S(1)}, bf16[256,512]{1,0:T(8,128)(2,1)S(1)}, u32[]{:S(2)}, u32[]{:S(2)}) collective-permute-start(bf16[256,512]{1,0:T(8,128)(2,1)S(1)} %get-tuple-element.40), channel_id=1, source_target_pairs={{0,24},{8,0},{16,8},{24,16},{32,56},{40,32},{48,40},{56,48},{64,88... | collective-permute-start | bytes 786440 | tf_op jit(solution)/shard_map/ppermute | solution.py:493
  74.7 14.4 %collective-permute-start.22 = (bf16[256,512]{1,0:T(8,128)(2,1)S(1)}, bf16[256,512]{1,0:T(8,128)(2,1)S(1)}, u32[]{:S(2)}, u32[]{:S(2)}) collective-permute-start(bf16[256,512]{1,0:T(8,128)(2,1)S(1)} %get-tuple-element.49), channel_id=1, source_target_pairs={{0,6},{1,7},{2,0},{3,1},{4,2},{5,3},{6,4},{7,5},{8,14},{9,15},{10,... | collective-permute-start | bytes 786440 | tf_op jit(solution)/shard_map/ppermute | solution.py:537
  77.4 11.6 %collective-permute-start.21 = (bf16[256,512]{1,0:T(8,128)(2,1)S(1)}, bf16[256,512]{1,0:T(8,128)(2,1)S(1)}, u32[]{:S(2)}, u32[]{:S(2)}) collective-permute-start(bf16[256,512]{1,0:T(8,128)(2,1)S(1)} %get-tuple-element.50), channel_id=1, source_target_pairs={{0,4},{1,5},{2,6},{3,7},{4,0},{5,1},{6,2},{7,3},{8,12},{9,13},{10,... | collective-permute-start | bytes 786440 | tf_op jit(solution)/shard_map/ppermute | solution.py:537
  80.4 12.4 %collective-permute-start.20 = (bf16[256,512]{1,0:T(8,128)(2,1)S(1)}, bf16[256,512]{1,0:T(8,128)(2,1)S(1)}, u32[]{:S(2)}, u32[]{:S(2)}) collective-permute-start(bf16[256,512]{1,0:T(8,128)(2,1)S(1)} %get-tuple-element.48), channel_id=1, source_target_pairs={{0,2},{1,3},{2,4},{3,5},{4,6},{5,7},{6,0},{7,1},{8,10},{9,11},{10,... | collective-permute-start | bytes 786440 | tf_op jit(solution)/shard_map/ppermute | solution.py:537
